TPU v7x, 32 devices: a whole 2x2x4 slice. The times are simulated.
32 devices in a mesh: row: 4 (over z), col: 8 (over y, x, core).
Axes of the slice: x: 2, y: 2, z: 4, core: 2. Of those that a mesh axis runs over, the one named last changes fastest.
Arguments:
- a_held: float32 [1024, 128, 128], P(('row', 'col')), may hold values from -0.5 to 0.5
- a_slot: int32 [1024], P(('row', 'col')), may hold values from 0 to 1023, as said below
- a_col: int32 [1024], P(('row', 'col')), may hold values from -1 to 15, as said below
- b_held: float32 [2048, 128, 128], P(('row', 'col')), may hold values from -6 to 6
- b_slot: int32 [2048], P(('row', 'col')), may hold values from 0 to 2047, as said below
- b_col: int32 [2048], P(('row', 'col')), may hold values from -1 to 15, as said below
- c_col: int32 [64, 48], P('row', 'col'), may hold values from -1 to 15, as said below
Outputs:
- product: float32 [64, 48, 128, 128], P('row', 'col')
Inputs may be any that keep to these rules, and one draw needn't show every extreme that they name: `a_slot`: a permutation of 0 to 1023; one device holds at most 2 slots of one left panel, and some device holds exactly that many. `a_col`: the filled columns of one block row of a left panel are distinct; some block row of every panel has all 4 slots filled. `b_slot`: a permutation of 0 to 2047; one device holds at most 2 slots of one right panel, and some device holds exactly that many. `b_col`: the filled columns of one inner block row of a right panel are distinct; some block row of every panel has all 4 slots filled. `c_col`: the retained columns of one block row within one grid column are distinct, -1 marks an empty slot; every grid column has a block row with all 6 slots retained.
All inputs are finite; a program needn't handle non-finite values.
Results may differ from a plain program's by a relative error of at most 0.0003.
Values sent between devices are 32-bit elements; how exact they have to be, the bound alone decides.
No kernel may reach another device: no remote copies, remote signals or barrier semaphores. Data moves between devices by JAX's collectives and lax.ppermute only.
A program may use at most 192 MiB of HBM per device.

v0:
```python
import jax
import jax.numpy as jnp
from jax import lax
from jax.sharding import PartitionSpec as P

KPB = 16
WA = 4
WB = 4
STEPS = 3


def shifted(value, axis, steps):
    count = lax.axis_size(axis)
    pairs = [(source, (source + steps) % count) for source in range(count)]
    return lax.ppermute(value, axis, pairs)


def route_matrix(dests, capacity, devices_all):
    flat_dest = dests.reshape(-1)
    position = jnp.arange(flat_dest.shape[0])
    before = (flat_dest[:, None] == flat_dest[None, :]) & (position[:, None] > position[None, :])
    rank_dest = jnp.sum(before.astype(jnp.int32), axis=1)
    target = flat_dest * capacity + rank_dest
    onehot_matrix = (target[None, :] == jnp.arange(devices_all * capacity)[:, None]).astype(
        jnp.float32
    )
    return onehot_matrix.reshape(devices_all * capacity, dests.shape[0], dests.shape[1]).sum(axis=2)


def pack_blocks(held_blocks, local_slot, column_indices, dests, capacity, devices_all):
    select = route_matrix(dests, capacity, devices_all)
    edge = held_blocks.shape[1]
    block_list = jnp.dot(
        select, held_blocks.reshape(held_blocks.shape[0], -1), precision=lax.Precision.HIGHEST
    )
    block_labels = jnp.stack(
        [
            local_slot.astype(jnp.float32),
            column_indices.astype(jnp.float32),
            jnp.ones(local_slot.shape, jnp.float32),
        ],
        axis=1,
    )
    marker_flags = jnp.dot(select, block_labels, precision=lax.Precision.HIGHEST)
    return (block_list.reshape(-1, edge, edge), marker_flags)


def expand_block_list(block_list, marker_flags, slot_count):
    present_flags = marker_flags[:, 2] > 0.5
    slot_location = marker_flags[:, 0].astype(jnp.int32)
    onehot_matrix = (
        (slot_location[None, :] == jnp.arange(slot_count)[:, None]) & present_flags[None, :]
    ).astype(jnp.float32)
    placed = jnp.dot(
        onehot_matrix, block_list.reshape(block_list.shape[0], -1), precision=lax.Precision.HIGHEST
    )
    filled = jnp.sum(onehot_matrix, axis=1) > 0.5
    block_labels = jnp.where(
        filled, jnp.dot(onehot_matrix, marker_flags[:, 1], precision=lax.Precision.HIGHEST), -1.0
    )
    return (placed, block_labels)


def panel_products(left, left_labels, right, right_labels, kept):
    left_cols = left_labels.astype(jnp.int32)
    safe = jnp.maximum(left_cols, 0)
    chosen = jnp.take(right, safe, axis=0)
    chosen_cols = jnp.take(right_labels, safe, axis=0).astype(jnp.int32)
    match = (
        (left_cols >= 0)[:, None, :, None]
        & (chosen_cols[:, None, :, :] == kept[:, :, None, None])
        & (kept >= 0)[:, :, None, None]
    )
    match = match.astype(jnp.float32)
    pieces = jnp.einsum("rwij,rwvjl->rwvil", left, chosen, precision=lax.Precision.HIGHEST)
    return jnp.einsum("rtwv,rwvil->rtil", match, pieces, precision=lax.Precision.HIGHEST)


def on_device(a_held, a_slot, a_col, b_held, b_slot, b_col, c_col):
    grid_rows = lax.axis_size("row")
    grid_cols = lax.axis_size("col")
    devices_all = grid_rows * grid_cols
    rows_dev = c_col.shape[0]
    retained_width = c_col.shape[1]
    edge = a_held.shape[1]
    slots_left = rows_dev * WA
    slots_right = KPB * WB
    capacity_left = max(1, slots_left // devices_all)
    capacity_right = max(1, slots_right // devices_all)
    copies = grid_cols // grid_rows
    panel_left = a_slot // slots_left
    left_grid_row = panel_left // grid_rows
    left_inner = panel_left % grid_rows
    first_col = (left_inner - left_grid_row) % grid_rows
    dest_left = (left_grid_row * grid_cols + first_col)[:, None] + grid_rows * jnp.arange(
        copies, dtype=jnp.int32
    )[None, :]
    panel_right = b_slot // slots_right
    right_inner = panel_right // grid_cols
    right_grid_col = panel_right % grid_cols
    dest_right = ((right_inner - right_grid_col) % grid_rows * grid_cols + right_grid_col)[:, None]
    send_left, marker_left = pack_blocks(
        a_held, a_slot % slots_left, a_col, dest_left, capacity_left, devices_all
    )
    send_right, marker_right = pack_blocks(
        b_held, b_slot % slots_right, b_col, dest_right, capacity_right, devices_all
    )
    recv_left, rmark_left, recv_right, rmark_right = (
        lax.all_to_all(send_left, ("row", "col"), split_axis=0, concat_axis=0, tiled=True),
        lax.all_to_all(marker_left, ("row", "col"), split_axis=0, concat_axis=0, tiled=True),
        lax.all_to_all(send_right, ("row", "col"), split_axis=0, concat_axis=0, tiled=True),
        lax.all_to_all(marker_right, ("row", "col"), split_axis=0, concat_axis=0, tiled=True),
    )
    left_flat, left_labels = expand_block_list(recv_left, rmark_left, slots_left)
    left_home = left_flat.reshape(rows_dev, WA, edge, edge)
    left_labels = left_labels.reshape(rows_dev, WA)
    right_flat, right_labels = expand_block_list(recv_right, rmark_right, slots_right)
    right_home = right_flat.reshape(KPB, WB, edge, edge)
    right_labels = right_labels.reshape(KPB, WB)
    accum = jnp.zeros((rows_dev, retained_width, edge, edge), jnp.float32)
    for iteration in range(STEPS):
        accum = accum + panel_products(left_home, left_labels, right_home, right_labels, c_col)
        if iteration + 1 < STEPS:
            left_home, left_labels = shifted((left_home, left_labels), "col", -1)
            right_home, right_labels = shifted((right_home, right_labels), "row", -1)
    return accum


def solution(mesh):
    return jax.shard_map(
        on_device,
        mesh=mesh,
        in_specs=(
            P(("row", "col"), None, None),
            P(("row", "col")),
            P(("row", "col")),
            P(("row", "col"), None, None),
            P(("row", "col")),
            P(("row", "col")),
            P("row", "col"),
        ),
        out_specs=P("row", "col", None, None),
        check_vma=False,
    )
```

profile of v0, /device:TPU:2, one launch (start us, length us, event | category | flops | bytes accessed | tf_op | source)
XLA Modules:
  0.0 660.9 jit_solution(4928122504345844931)
XLA Ops:
  2.4 6.1 all-to-all-start.1
  18.2 6.8 %fusion.25 = f32[64,128,128]{2,0,1:T(8,128)S(1)} fusion(s32[64]{0:T(128)S(1)} %multiply_add_fusion.2, f32[8,8,128,128]{3,2,1,0:T(8,128)} %bitcast.152), kind=kOutput, calls=%fused_computation.32 | convolution fusion | flops 805310464 | bytes 8388864 | tf_op jit(solution)/shard_map/dot_general | solution.py:33
  25.1 4.4 copy.142
  29.5 6.4 all-to-all-start.2
  35.9 4.6 fusion.31
  40.6 4.4 copy.147
  44.9 84.3 %all-to-all-done.2 = f32[64,128,128]{2,1,0:T(8,128)} async-done(((f32[64,128,128]{2,1,0:T(8,128)}), f32[64,128,128]{2,1,0:T(8,128)}, u32[]{:S(2)}, u32[]{:S(2)}) %all-to-all-start.2) | async-done | bytes 4194336 | tf_op jit(solution)/shard_map/all_to_all | solution.py:111
  129.2 4.5 all-to-all-start.3
  134.3 8.9 %fusion.23 = f32[16,4,128,128]{3,0,2,1:T(8,128)} fusion(s32[16,4]{0,1:T(4,128)S(1)} %multiply_add_fusion.1, s32[64]{0:T(128)S(1)} %bitcast.164, pred[64]{0:T(512)(128)(4,1)S(1)} %bitcast.170, f32[8,8,128,128]{3,2,1,0:T(8,128)} %bitcast.70), kind=kOutput, calls=%fused_computation.30 | convolution fusion | flops 805314560 | bytes 8389184 | tf_op jit(solution)/shard_map/dot_general | solution.py:54
  146.9 80.9 %all-to-all-done.3 = f32[64,128,128]{2,1,0:T(8,128)} async-done(((f32[64,128,128]{2,1,0:T(8,128)}), f32[64,128,128]{2,1,0:T(8,128)}, u32[]{:S(2)}, u32[]{:S(2)}) %all-to-all-start.3) | async-done | bytes 4194336 | tf_op jit(solution)/shard_map/all_to_all | solution.py:109
  227.8 8.9 %fusion.21 = f32[16,4,128,128]{3,0,2,1:T(8,128)} fusion(s32[64]{0:T(128)S(1)} %bitcast.167, s32[16,4]{0,1:T(4,128)S(1)} %multiply_add_fusion.1, pred[64]{0:T(512)(128)(4,1)S(1)} %bitcast.173, f32[8,8,128,128]{3,2,1,0:T(8,128)} %bitcast.74), kind=kOutput, calls=%fused_computation.27 | convolution fusion | flops 805314560 | bytes 8389184 | tf_op jit(solution)/shard_map/dot_general | solution.py:54
  238.8 91.3 %collective-permute-start.1 = (f32[16,4]{1,0:T(8,128)S(1)}, f32[16,4]{1,0:T(8,128)S(1)}, u32[]{:S(2)}, u32[]{:S(2)}) collective-permute-start(f32[16,4]{1,0:T(8,128)S(1)} %reshape.184), channel_id=1, source_target_pairs={{0,24},{8,0},{16,8},{24,16},{1,25},{9,1},{17,9},{25,17},{2,26},{10... | collective-permute-start | bytes 776 | tf_op jit(solution)/shard_map/ppermute | solution.py:15
  333.7 44.1 %collective-permute-start.5 = (f32[16,4]{1,0:T(8,128)S(1)}, f32[16,4]{1,0:T(8,128)S(1)}, u32[]{:S(2)}, u32[]{:S(2)}) collective-permute-start(f32[16,4]{1,0:T(8,128)S(1)} %collective-permute-done.1), channel_id=1, source_target_pairs={{0,24},{8,0},{16,8},{24,16},{1,25},{9,1},{17,9},{25,17},{2,26},{10... | collective-permute-start | bytes 776 | tf_op jit(solution)/shard_map/ppermute | solution.py:15
  380.1 5.5 copy.144
  385.6 11.0 %gather_fusion.1 = f32[64,4,128,128]{3,2,1,0:T(8,128)} fusion(f32[16,4,128,128]{3,2,1,0:T(8,128)} %copy.144, s32[1024]{0:T(1024)S(1)} %pad_clamp_fusion.2), kind=kCustom, calls=%fused_computation.1.clone | custom fusion | bytes 33554688 | tf_op jit(solution)/shard_map/jit(_take)/gather | solution.py:67
  396.6 17.6 %copy.145 = f32[16,4,4,128,128]{3,4,2,1,0:T(8,128)} copy(f32[16,4,4,128,128]{4,3,2,1,0:T(8,128)} %bitcast.149) | data formatting | bytes 33554432 | tf_op jit(solution)/shard_map/jit(_take)/gather | solution.py:67
  414.2 4.1 collective-permute-start.6
  418.5 20.4 %fusion.6 = f32[16,4,4,128,128]{3,4,2,1,0:T(8,128)} fusion(f32[16,4,4,128,128]{3,4,2,1,0:T(8,128)} %copy.145, pred[16,4]{1,0:T(8,128)(4,1)S(1)} %get-tuple-element.10, f32[16,4,128,128,1]{3,0,2,1,4:T(8,128)} %bitcast.33), kind=kOutput, calls=%fused_computation.12 | convolution fusion | flops 6446645248 | bytes 37748800 | tf_op jit(solution)/shard_map/rwij,rwvjl->rwvil/dot_general | solution.py:75
  438.8 19.8 %copy.150 = f32[16,4,4,128,128]{4,1,2,3,0:T(4,128)} copy(f32[16,4,4,128,128]{3,4,2,1,0:T(8,128)} %fusion.6) | data formatting | bytes 33554432 | tf_op jit(solution)/shard_map/rwij,rwvjl->rwvil/transpose | solution.py:75
  458.7 16.0 %fusion.39 = f32[16,6,128,128,1]{3,1,4,2,0:T(8,128)} fusion(f32[16,4,4,128,128]{4,1,2,3,0:T(4,128)} %copy.150, s32[16,6]{1,0:T(8,128)S(1)} %copy.139, s32[16,4,4]{1,2,0:T(4,128)S(1)} %copy.138, pred[16,6]{1,0:T(8,128)(4,1)S(1)} %copy.140, pred[16,4]{1,0:T(8,128)(4,1)S(1)} %get-tuple-element.9), kind=kOutput, calls=%fused_computation.49 | convolution fusion | flops 301994496 | bytes 23070240 | tf_op jit(solution)/shard_map/rtwv,rwvil->rtil/dot_general | solution.py:76
  474.7 5.5 copy.155
  480.3 11.0 %gather_fusion.3 = f32[64,4,128,128]{3,2,1,0:T(8,128)} fusion(f32[16,4,128,128]{3,2,1,0:T(8,128)} %copy.155, s32[1024]{0:T(1024)S(1)} %pad_clamp_fusion.1), kind=kCustom, calls=%fused_computation.4.clone | custom fusion | bytes 33554688 | tf_op jit(solution)/shard_map/jit(_take)/gather | solution.py:67
  491.2 17.6 %copy.156 = f32[16,4,4,128,128]{3,4,2,1,0:T(8,128)} copy(f32[16,4,4,128,128]{4,3,2,1,0:T(8,128)} %bitcast.150) | data formatting | bytes 33554432 | tf_op jit(solution)/shard_map/jit(_take)/gather | solution.py:67
  508.9 20.6 %fusion.9 = f32[16,4,4,128,128]{3,4,2,1,0:T(8,128)} fusion(f32[16,4,4,128,128]{3,4,2,1,0:T(8,128)} %copy.156, pred[16,4]{1,0:T(8,128)(4,1)S(1)} %get-tuple-element.12, f32[16,4,128,128,1]{3,0,2,1,4:T(8,128)} %bitcast.41), kind=kOutput, calls=%fused_computation.13 | convolution fusion | flops 6446645248 | bytes 37748800 | tf_op jit(solution)/shard_map/rwij,rwvjl->rwvil/dot_general | solution.py:75
  529.4 19.8 %copy.158 = f32[16,4,4,128,128]{4,1,2,3,0:T(4,128)} copy(f32[16,4,4,128,128]{3,4,2,1,0:T(8,128)} %fusion.9) | data formatting | bytes 33554432 | tf_op jit(solution)/shard_map/rwij,rwvjl->rwvil/transpose | solution.py:75
  549.2 16.0 %fusion.37 = f32[16,6,128,128,1]{3,1,4,2,0:T(8,128)} fusion(f32[16,4,4,128,128]{4,1,2,3,0:T(4,128)} %copy.158, s32[16,4,4]{1,2,0:T(4,128)S(1)} %copy.154, s32[16,6]{1,0:T(8,128)S(1)} %copy.139, pred[16,4]{1,0:T(8,128)(4,1)S(1)} %get-tuple-element.11, pred[16,6]{1,0:T(8,128)(4,1)S(1)} %copy.140), kind=kOutput, calls=%fused_computation.47 | convolution fusion | flops 301994496 | bytes 23070240 | tf_op jit(solution)/shard_map/rtwv,rwvil->rtil/dot_general | solution.py:76
  565.3 5.6 copy.163
  570.8 11.0 %gather_fusion.5 = f32[64,4,128,128]{3,2,1,0:T(8,128)} fusion(f32[16,4,128,128]{3,2,1,0:T(8,128)} %copy.163, s32[1024]{0:T(1024)S(1)} %pad_clamp_fusion), kind=kCustom, calls=%fused_computation.5.clone | custom fusion | bytes 33554688 | tf_op jit(solution)/shard_map/jit(_take)/gather | solution.py:67
  581.8 17.6 %copy.164 = f32[16,4,4,128,128]{3,4,2,1,0:T(8,128)} copy(f32[16,4,4,128,128]{4,3,2,1,0:T(8,128)} %bitcast.151) | data formatting | bytes 33554432 | tf_op jit(solution)/shard_map/jit(_take)/gather | solution.py:67
  599.5 20.6 %fusion.12 = f32[16,4,4,128,128]{3,4,2,1,0:T(8,128)} fusion(f32[16,4,4,128,128]{3,4,2,1,0:T(8,128)} %copy.164, pred[16,4]{1,0:T(8,128)(4,1)S(1)} %get-tuple-element.8, f32[16,4,128,128,1]{3,0,2,1,4:T(8,128)} %bitcast.49), kind=kOutput, calls=%fused_computation.14 | convolution fusion | flops 6446645248 | bytes 37748800 | tf_op jit(solution)/shard_map/rwij,rwvjl->rwvil/dot_general | solution.py:75
  620.1 19.8 %copy.166 = f32[16,4,4,128,128]{4,1,2,3,0:T(4,128)} copy(f32[16,4,4,128,128]{3,4,2,1,0:T(8,128)} %fusion.12) | data formatting | bytes 33554432 | tf_op jit(solution)/shard_map/rwij,rwvjl->rwvil/transpose | solution.py:75
  639.9 16.8 %bitcast_add_fusion = f32[16,6,128,128]{3,1,2,0:T(8,128)S(1)} fusion(f32[16,6,128,128,1]{3,1,4,2,0:T(8,128)} %fusion.37, f32[16,6,128,128,1]{3,1,4,2,0:T(8,128)} %fusion.39, f32[16,4,4,128,128]{4,1,2,3,0:T(4,128)} %copy.166, s32[16,4,4]{1,2,0:T(4,128)S(1)} %copy.162, s32[16,6]{1,0:T(8,128)S(1)} %copy.139, pred[16,4]{1,0:T(8,128)(4,1)S(1)} %get-tuple-element.6, ...), kind=kOutput, calls=%fused_computation.15 | convolution fusion | flops 305140224 | bytes 35653152 | tf_op jit(solution)/shard_map/rtwv,rwvil->rtil/dot_general | solution.py:76
  (85 shorter events, 28.1 us)
Async XLA Ops:
  2.4 12.1 %all-to-all-start.1 = ((f32[32,2,3]{2,1,0:T(2,128)}), f32[32,2,3]{2,1,0:T(2,128)S(1)}, u32[]{:S(2)}, u32[]{:S(2)}) async-start(f32[32,2,3]{2,1,0:T(2,128)} %bitcast.11), calls=%async_computation.1 | async-start | bytes 65536 | tf_op jit(solution)/shard_map/all_to_all | solution.py:112
  14.5 15.0 %all-to-all-start = ((f32[32,2,3]{2,1,0:T(2,128)}), f32[32,2,3]{2,1,0:T(2,128)S(1)}, u32[]{:S(2)}, u32[]{:S(2)}) async-start(f32[32,2,3]{2,1,0:T(2,128)} %copy.131), calls=%async_computation | async-start | bytes 65536 | tf_op jit(solution)/shard_map/all_to_all | solution.py:110
  29.5 6.4 copy-start
  29.5 99.7 %all-to-all-start.2 = ((f32[64,128,128]{2,1,0:T(8,128)}), f32[64,128,128]{2,1,0:T(8,128)}, u32[]{:S(2)}, u32[]{:S(2)}) async-start(f32[64,128,128]{2,1,0:T(8,128)} %copy.142), calls=%async_computation.2 | async-start | bytes 8388608 | tf_op jit(solution)/shard_map/all_to_all | solution.py:111
  129.2 98.6 %all-to-all-start.3 = ((f32[64,128,128]{2,1,0:T(8,128)}), f32[64,128,128]{2,1,0:T(8,128)}, u32[]{:S(2)}, u32[]{:S(2)}) async-start(f32[64,128,128]{2,1,0:T(8,128)} %copy.147), calls=%async_computation.3 | async-start | bytes 8388608 | tf_op jit(solution)/shard_map/all_to_all | solution.py:109
  143.2 271.0 %collective-permute-start.2 = (f32[16,4,128,128]{3,0,2,1:T(8,128)}, f32[16,4,128,128]{3,0,2,1:T(8,128)}, u32[]{:S(2)}, u32[]{:S(2)}) collective-permute-start(f32[16,4,128,128]{3,0,2,1:T(8,128)} %fusion.23), channel_id=1, source_target_pairs={{0,24},{8,0},{16,8},{24,16},{1,25},{9,1},{17,9},{25,17},{2,26},{10... | collective-permute-start | bytes 12582920 | tf_op jit(solution)/shard_map/ppermute | solution.py:15
  227.8 9.0 %copy-start.1 = (s32[16,6]{0,1:T(8,128)S(1)}, s32[16,6]{0,1:T(8,128)}, u32[]{:S(2)}) copy-start(s32[16,6]{0,1:T(8,128)} %param.17) | copy-start | bytes 1156
  236.7 181.6 %collective-permute-start.3 = (f32[16,4,128,128]{3,0,2,1:T(8,128)}, f32[16,4,128,128]{3,0,2,1:T(8,128)}, u32[]{:S(2)}, u32[]{:S(2)}) collective-permute-start(f32[16,4,128,128]{3,0,2,1:T(8,128)} %fusion.21), channel_id=1, source_target_pairs={{0,7},{1,0},{2,1},{3,2},{4,3},{5,4},{6,5},{7,6},{8,15},{9,8},{10,9... | collective-permute-start | bytes 12582920 | tf_op jit(solution)/shard_map/ppermute | solution.py:15
  237.4 93.8 %collective-permute-start = (f32[16,4]{1,0:T(8,128)S(1)}, f32[16,4]{1,0:T(8,128)S(1)}, u32[]{:S(2)}, u32[]{:S(2)}) collective-permute-start(f32[16,4]{1,0:T(8,128)S(1)} %reshape.183), channel_id=1, source_target_pairs={{0,7},{1,0},{2,1},{3,2},{4,3},{5,4},{6,5},{7,6},{8,15},{9,8},{10,9... | collective-permute-start | bytes 776 | tf_op jit(solution)/shard_map/ppermute | solution.py:15
  238.8 92.7 %collective-permute-start.1 = (f32[16,4]{1,0:T(8,128)S(1)}, f32[16,4]{1,0:T(8,128)S(1)}, u32[]{:S(2)}, u32[]{:S(2)}) collective-permute-start(f32[16,4]{1,0:T(8,128)S(1)} %reshape.184), channel_id=1, source_target_pairs={{0,24},{8,0},{16,8},{24,16},{1,25},{9,1},{17,9},{25,17},{2,26},{10... | collective-permute-start | bytes 776 | tf_op jit(solution)/shard_map/ppermute | solution.py:15
  332.3 45.5 %collective-permute-start.4 = (f32[16,4]{1,0:T(8,128)S(1)}, f32[16,4]{1,0:T(8,128)S(1)}, u32[]{:S(2)}, u32[]{:S(2)}) collective-permute-start(f32[16,4]{1,0:T(8,128)S(1)} %collective-permute-done), channel_id=1, source_target_pairs={{0,7},{1,0},{2,1},{3,2},{4,3},{5,4},{6,5},{7,6},{8,15},{9,8},{10,9... | collective-permute-start | bytes 776 | tf_op jit(solution)/shard_map/ppermute | solution.py:15
  333.7 45.5 %collective-permute-start.5 = (f32[16,4]{1,0:T(8,128)S(1)}, f32[16,4]{1,0:T(8,128)S(1)}, u32[]{:S(2)}, u32[]{:S(2)}) collective-permute-start(f32[16,4]{1,0:T(8,128)S(1)} %collective-permute-done.1), channel_id=1, source_target_pairs={{0,24},{8,0},{16,8},{24,16},{1,25},{9,1},{17,9},{25,17},{2,26},{10... | collective-permute-start | bytes 776 | tf_op jit(solution)/shard_map/ppermute | solution.py:15
  414.2 151.1 %collective-permute-start.6 = (f32[16,4,128,128]{3,0,2,1:T(8,128)}, f32[16,4,128,128]{3,0,2,1:T(8,128)}, u32[]{:S(2)}, u32[]{:S(2)}) collective-permute-start(f32[16,4,128,128]{3,0,2,1:T(8,128)} %collective-permute-done.2), channel_id=1, source_target_pairs={{0,24},{8,0},{16,8},{24,16},{1,25},{9,1},{17,9},{25,17},{2,26},{10... | collective-permute-start | bytes 12582920 | tf_op jit(solution)/shard_map/ppermute | solution.py:15
  418.3 181.2 %collective-permute-start.7 = (f32[16,4,128,128]{3,0,2,1:T(8,128)}, f32[16,4,128,128]{3,0,2,1:T(8,128)}, u32[]{:S(2)}, u32[]{:S(2)}) collective-permute-start(f32[16,4,128,128]{3,0,2,1:T(8,128)} %collective-permute-done.3), channel_id=1, source_target_pairs={{0,7},{1,0},{2,1},{3,2},{4,3},{5,4},{6,5},{7,6},{8,15},{9,8},{10,9... | collective-permute-start | bytes 12582920 | tf_op jit(solution)/shard_map/ppermute | solution.py:15
where the time goes:
time: 673 us; the launch traced here: 661 us
  local copies, waits for them, and re-layouts  179 us (27%)
  waiting for transfers between devices  169 us (25%)
  starting transfers between devices  166 us (25%)
  matrix products  141 us (21%)
    ppermute x8, starting transfers between devices, shifted(): return lax.ppermute(value, axis, pairs)  146 us
    gather x6, local copies, waits for them, and re-layouts, panel_products(): chosen = jnp.take(right, safe, axis=0)  85.8 us
    all_to_all x1, waiting for transfers between devices, on_device(): lax.all_to_all(send_right, ('row', 'col'), split_axis=0, concat_axis=0, t...  84.3 us
    all_to_all x1, waiting for transfers between devices, on_device(): lax.all_to_all(send_left, ('row', 'col'), split_axis=0, concat_axis=0, ti...  80.9 us
    dot_general x3, matrix products, panel_products(): jnp.einsum('rwij,rwvjl->rwvil', left, chosen, precision=lax.Precision.HIG...  61.6 us
    transpose x3, local copies, waits for them, and re-layouts, panel_products(): jnp.einsum('rwij,rwvjl->rwvil', left, chosen, precision=lax.Precision.HIG...  59.4 us
    dot_general x3, matrix products, panel_products(): jnp.einsum('rtwv,rwvil->rtil', match, pieces, precision=lax.Precision.HIG...  48.9 us
    dot_general x2, matrix products, expand_block_list(): jnp.dot(onehot_matrix, block_list.reshape(block_list.shape[0], -1), preci...  17.8 us
  transfers between devices with their start and end apart: 12, of which 5 were waited for; matrix products, arithmetic and copies ran while one was open for 39% of the time, Pallas kernels for 0%

commit v1 on v0

v1 whole, which is shorter than its diff:
```python
import functools

import jax
import jax.numpy as jnp
import numpy as np
from jax import lax
from jax.experimental import pallas as pl
from jax.experimental.pallas import tpu as pltpu
from jax.sharding import PartitionSpec as P

KPB = 16
WA = 4
WB = 4
STEPS = 3
LABEL = 32
ROUNDS = (24,) * 5
LAG = 1
STAGE = 3
FAR = 1 << 16
LOOP_ROUND = 8
SLOTS = 8
VMEM_BYTES = 56 * 2**20


def swap(value, axis, distance):
    if distance == 0:
        return value
    count = lax.axis_size(axis)
    return lax.ppermute(value, axis, [(at, at ^ distance) for at in range(count)])


def share(values):
    count = lax.axis_size("row") * lax.axis_size("col")
    sent = jnp.broadcast_to(values[None], (count,) + values.shape)
    return lax.all_to_all(sent, ("row", "col"), split_axis=0, concat_axis=0, tiled=True)


def pack_order(panel_at, slot, column, places):
    position = jnp.arange(panel_at.shape[0])
    same = (panel_at[:, None] == panel_at[None, :]) & (position[:, None] > position[None, :])
    place = panel_at + jnp.sum(same.astype(jnp.int32), axis=1)
    hit = place[None, :] == jnp.arange(places)[:, None]
    entry = jnp.sum(jnp.where(hit, position[None, :], 0), axis=1)
    label = jnp.sum(jnp.where(hit, (slot * LABEL + column + 2)[None, :], 0), axis=1) - 1
    return entry, label


def split_label(label):
    return jnp.where(label >= 0, label // LABEL, -1), jnp.where(label >= 0, label % LABEL - 1, -1)


def locate(place, bounds):
    part = jnp.zeros(place.shape, jnp.int32)
    offset = place
    for at in range(1, len(bounds) - 1):
        part = part + (place >= int(bounds[at]))
        offset = offset - jnp.where(place >= int(bounds[at]), int(bounds[at] - bounds[at - 1]), 0)
    return part, offset


def flags(condition):
    return condition.astype(jnp.bfloat16)


def starts_of(sizes):
    return np.concatenate([[0], np.cumsum(sizes)]).astype(int)


def available(place, sizes, lag):
    starts = starts_of(sizes)
    ready = jnp.full(place.shape, int(starts[min(lag, len(sizes))]), jnp.int32)
    for at in range(1, len(sizes)):
        gain = int(starts[min(at + lag, len(sizes))] - starts[min(at + lag - 1, len(sizes))])
        if gain:
            ready = ready + jnp.where(place >= int(starts[at]), gain, 0)
    return jnp.where(place >= int(starts[max(len(sizes) - lag, 0)]), FAR, ready)


def one_turn(function, values):
    empty = jax.tree.map(
        lambda part: jnp.zeros(part.shape, part.dtype), jax.eval_shape(function, values)
    )
    turns = 1 + jnp.minimum(jnp.max(values) + 1, 0)
    return lax.fori_loop(0, turns, lambda at, carry: function(values + at), empty)


def queue_places(wanted, origin, ready):
    count, entries = wanted.shape[1:]
    reach = jnp.max(jnp.where(wanted, jnp.arange(count)[None, :, None], -1), axis=1)
    key = ((count - 1 - reach) * count + (count - 1 - origin)) * entries + jnp.arange(entries)
    earlier = key[:, :, None] < key[:, None, :]
    link = jnp.arange(count - 1)[None, :, None]
    item = (origin[:, None] <= link) & (reach[:, None] > link)
    rank = jnp.einsum(
        "dle,def->dlf", flags(item), flags(earlier), preferred_element_type=jnp.float32
    ).astype(jnp.int32)
    upto = earlier | jnp.eye(entries, dtype=bool)[None]
    place = rank[:, 0]
    places = [place]
    for at in range(1, count - 1):
        relayed = item[:, at] & (origin < at)
        behind = jnp.where(relayed, ready(place) - rank[:, at], 0)
        delay = jnp.max(jnp.where(upto, behind[:, :, None], 0), axis=1)
        place = rank[:, at] + delay
        places.append(place)
    return jnp.where(item, jnp.stack(places, axis=1), -1)


def choose(refs, which, use):
    if len(refs) == 1:
        use(refs[0])
        return
    half = len(refs) // 2

    @pl.when(which < half)
    def _():
        choose(refs[:half], which, use)

    @pl.when(which >= half)
    def _():
        choose(refs[half:], which - half, use)


def copy_costs(blocks, edge):
    return pl.CostEstimate(flops=0, bytes_accessed=2 * blocks * edge * edge * 4, transcendentals=0)


def local_params():
    return pltpu.CompilerParams(vmem_limit_bytes=VMEM_BYTES)


def relay(load, outs, buf, load_sem, store_sem):
    total = buf.shape[0]
    lax.fori_loop(
        0, total, lambda at, carry: (load(at, buf.at[at], load_sem.at[at]), carry)[1], 0
    )
    place = 0
    for out in outs:

        def one(at, carry, out=out, place=place):
            pltpu.make_async_copy(
                buf.at[place + at], buf.at[place + at], load_sem.at[place + at]
            ).wait()
            pltpu.make_async_copy(buf.at[place + at], out.at[at], store_sem).start()
            return carry

        lax.fori_loop(0, out.shape[0], one, 0)
        place += out.shape[0]
    for out in outs:
        pltpu.make_async_copy(out, out, store_sem).wait()


def relay_call(kernel, name, codes, sources, sizes):
    block = sources[0].shape[1:]
    total = sum(sizes)
    hbm = pl.BlockSpec(memory_space=pltpu.HBM)
    return pl.pallas_call(
        kernel,
        out_shape=[jax.ShapeDtypeStruct((size,) + block, jnp.float32) for size in sizes],
        in_specs=[pl.BlockSpec(memory_space=pltpu.SMEM)] + [hbm] * len(sources),
        out_specs=[hbm] * len(sizes),
        scratch_shapes=[
            pltpu.VMEM((total,) + block, jnp.float32),
            pltpu.SemaphoreType.DMA((total,)),
            pltpu.SemaphoreType.DMA,
        ],
        compiler_params=local_params(),
        cost_estimate=copy_costs(0, block[0]),
        name=name,
    )(codes, *sources)


def sort_kernel(counts, index_ref, *refs):
    (first, second), outs, (buf, load_sem, store_sem) = refs[:2], refs[2:-3], refs[-3:]

    def load(at, target, sem):
        index = index_ref[at]

        @pl.when(at < counts)
        def _():
            pltpu.make_async_copy(first.at[index], target, sem).start()

        @pl.when(at >= counts)
        def _():
            pltpu.make_async_copy(second.at[index], target, sem).start()

    relay(load, outs, buf, load_sem, store_sem)


def sort_blocks(first, second, first_index, second_index):
    sizes = [index.shape[1] for index in (first_index, second_index) for _ in range(index.shape[0])]
    codes = jnp.concatenate([first_index.reshape(-1), second_index.reshape(-1)])
    kernel = functools.partial(sort_kernel, first_index.size)
    outs = relay_call(kernel, "sort_blocks", codes, [first, second], sizes)
    return list(outs[: first_index.shape[0]]), list(outs[first_index.shape[0] :])


def join_kernel(*refs):
    parts, (out, buf, load_sem, store_sem) = refs[:-4], refs[-4:]
    spans, place = [], 0
    for part in parts:
        spans.append(pl.ds(place, part.shape[0]))
        place += part.shape[0]
    loads = [
        pltpu.make_async_copy(part, buf.at[span], load_sem.at[at])
        for at, (part, span) in enumerate(zip(parts, spans))
    ]
    for load in loads:
        load.start()
    for load, span in zip(loads, spans):
        load.wait()
        pltpu.make_async_copy(buf.at[span], out.at[span], store_sem).start()
    pltpu.make_async_copy(out, out, store_sem).wait()


def join(parts):
    blocks = sum(part.shape[0] for part in parts)
    block = parts[0].shape[1:]
    hbm = pl.BlockSpec(memory_space=pltpu.HBM)
    return pl.pallas_call(
        join_kernel,
        out_shape=jax.ShapeDtypeStruct((blocks,) + block, jnp.float32),
        in_specs=[hbm] * len(parts),
        out_specs=hbm,
        scratch_shapes=[
            pltpu.VMEM((blocks,) + block, jnp.float32),
            pltpu.SemaphoreType.DMA((len(parts),)),
            pltpu.SemaphoreType.DMA,
        ],
        compiler_params=local_params(),
        cost_estimate=copy_costs(blocks, block[0]),
        name="join",
    )(*parts)


def pack_kernel(seen, size, index_ref, *refs):
    sources, outs, (buf, load_sem, store_sem) = refs[:-5], refs[-5:-3], refs[-3:]

    def load(at, target, sem):
        code = index_ref[at]

        def start(ref):
            pltpu.make_async_copy(ref.at[code & 127], target, sem).start()

        for side in range(2):

            @pl.when((at >= side * size) & (at < (side + 1) * size))
            def _():
                arrays = sources[:1] + sources[1 + side * seen : 1 + (side + 1) * seen]
                choose(arrays, lax.shift_right_logical(code, 7), start)

    relay(load, outs, buf, load_sem, store_sem)


def pack_round(codes, own, ups, downs):
    size = codes.shape[1]
    kernel = functools.partial(pack_kernel, len(ups), size)
    return relay_call(kernel, "pack_round", codes.reshape(-1), [own, *ups, *downs], [size, size])


def multiply_kernel(rights, first, list_ref, count_ref, a_ref, *refs):
    b_refs, refs = refs[:rights], refs[rights:]
    if not first:
        c_ref, refs = refs[0], refs[1:]
    out_ref, acc, a_buf, b_buf, a_sem, b_sem, c_sem = refs
    kept = out_ref.shape[0]
    count = count_ref[0]

    def fetch(at):
        @pl.when(at < count)
        def _():
            code = list_ref[at]
            slot = lax.rem(at, SLOTS)
            a_at = lax.shift_right_logical(code, 12) & 2047
            b_off = code & (4095 if rights == 1 else 127)
            pltpu.make_async_copy(a_ref.at[a_at], a_buf.at[slot], a_sem.at[slot]).start()

            def right(ref):
                pltpu.make_async_copy(ref.at[b_off], b_buf.at[slot], b_sem.at[slot]).start()

            choose(b_refs, lax.shift_right_logical(code, 7) & 31, right)

    lax.fori_loop(0, SLOTS, lambda at, carry: (fetch(at), carry)[1], 0)
    if first:

        def clear(at, carry):
            acc[at] = jnp.zeros(acc.shape[1:], jnp.float32)
            return carry

        lax.fori_loop(0, kept, clear, 0)
    else:
        load = pltpu.make_async_copy(c_ref, acc, c_sem)
        load.start()
        load.wait()

    def step(at, carry):
        slot = lax.rem(at, SLOTS)
        pltpu.make_async_copy(a_buf.at[slot], a_buf.at[slot], a_sem.at[slot]).wait()
        pltpu.make_async_copy(b_buf.at[slot], b_buf.at[slot], b_sem.at[slot]).wait()
        a = a_buf[slot]
        b = b_buf[slot]
        a_hi = a.astype(jnp.bfloat16)
        b_hi = b.astype(jnp.bfloat16)
        a_lo = (a - a_hi.astype(jnp.float32)).astype(jnp.bfloat16)
        b_lo = (b - b_hi.astype(jnp.float32)).astype(jnp.bfloat16)
        dot = functools.partial(jnp.dot, preferred_element_type=jnp.float32)
        target = lax.shift_right_logical(list_ref[at], 23)
        acc[target] += dot(a_hi, b_hi) + (dot(a_hi, b_lo) + dot(a_lo, b_hi))
        fetch(at + SLOTS)
        return carry

    lax.fori_loop(0, count, step, 0)
    store = pltpu.make_async_copy(acc, out_ref, c_sem)
    store.start()
    store.wait()


def multiply(codes, count, left, rights, kept, total=None):
    block = left.shape[1:]
    smem = pl.BlockSpec(memory_space=pltpu.SMEM)
    hbm = pl.BlockSpec(memory_space=pltpu.HBM)
    first = total is None
    arrays = [left, *rights] + ([] if first else [total])
    return pl.pallas_call(
        functools.partial(multiply_kernel, len(rights), first),
        out_shape=jax.ShapeDtypeStruct((kept,) + block, jnp.float32),
        in_specs=[smem, smem] + [hbm] * len(arrays),
        out_specs=hbm,
        scratch_shapes=[
            pltpu.VMEM((kept,) + block, jnp.float32),
            pltpu.VMEM((SLOTS,) + block, jnp.float32),
            pltpu.VMEM((SLOTS,) + block, jnp.float32),
            pltpu.SemaphoreType.DMA((SLOTS,)),
            pltpu.SemaphoreType.DMA((SLOTS,)),
            pltpu.SemaphoreType.DMA,
        ],
        compiler_params=local_params(),
        cost_estimate=pl.CostEstimate(
            flops=150 * 6 * block[0] ** 3, bytes_accessed=64 * 2**20, transcendentals=0
        ),
        name="multiply",
    )(codes, count, *arrays)


def hold_kernel(in_ref, out_ref):
    out_ref[...] = in_ref[...]


def hold(values):
    return pl.pallas_call(
        hold_kernel,
        out_shape=jax.ShapeDtypeStruct(values.shape, values.dtype),
        cost_estimate=pl.CostEstimate(flops=0, bytes_accessed=2**28, transcendentals=0),
        name="hold",
    )(values)


def compact(valid, codes):
    candidates = valid.shape[0]
    position = jnp.arange(candidates)
    before = flags(position[:, None] < position[None, :])
    place = jnp.dot(flags(valid)[None], before, preferred_element_type=jnp.float32)[0]
    hit = (place.astype(jnp.int32)[None, :] == position[:, None]) & valid[None, :]
    packed = jnp.sum(jnp.where(hit, codes[None, :], 0), axis=1)
    return packed, jnp.sum(valid.astype(jnp.int32)).reshape(1)


def on_device(a_held, a_slot, a_col, b_held, b_slot, b_col, c_col):
    grid_rows = lax.axis_size("row")
    grid_cols = lax.axis_size("col")
    devices_all = grid_rows * grid_cols
    row = lax.axis_index("row")
    col = lax.axis_index("col")
    rows_dev, retained_width = c_col.shape
    edge = a_held.shape[1]
    slots_left = rows_dev * WA
    slots_right = KPB * WB
    depth_left = max(1, slots_left // devices_all)
    depth_right = max(1, slots_right // devices_all)
    places_left = grid_rows * grid_rows * depth_left
    places_right = grid_cols * grid_rows * depth_right
    rows_at = jnp.arange(grid_rows)

    entry_left, label_left = pack_order(
        a_slot // slots_left * depth_left, a_slot % slots_left, a_col, places_left
    )
    panel_right = b_slot // slots_right
    entry_right, label_right = pack_order(
        (panel_right % grid_cols * grid_rows + panel_right // grid_cols) * depth_right,
        b_slot % slots_right,
        b_col,
        places_right,
    )
    entry_left = jnp.take(entry_left.reshape(grid_rows, -1), row ^ rows_at, axis=0)

    labels = share(jnp.concatenate([label_left, label_right, c_col.reshape(-1)]))

    sent_left, sent_right = sort_blocks(a_held, b_held, entry_left, entry_right[None])
    labels, *sent = lax.optimization_barrier((labels, *sent_left, *sent_right))
    home_right = lax.all_to_all(sent[-1], "col", split_axis=0, concat_axis=0, tiled=True)
    home = [swap(part, "row", at) for at, part in enumerate(sent[:-1])]
    local = home_right.shape[0]

    up = [(at, at + 1) for at in range(grid_rows - 1)]
    down = [(at + 1, at) for at in range(grid_rows - 1)]
    starts = starts_of(ROUNDS)
    capacity = int(starts[-1])
    shape = (grid_rows, grid_rows, grid_cols, depth_right)
    inner_of, origin, from_of, depth_of = (part.reshape(-1) for part in np.indices(shape))
    place_home = jnp.asarray((from_of * grid_rows + inner_of) * depth_right + depth_of, jnp.int32)
    origins = jnp.asarray(np.stack([origin, grid_rows - 1 - origin]), jnp.int32)
    self_at = jnp.stack([row, grid_rows - 1 - row])

    def split_labels(labels):
        left = labels[:, :places_left].reshape(
            grid_rows, grid_cols, grid_rows, grid_rows, depth_left
        )
        right = labels[:, places_left : places_left + places_right].reshape(
            grid_rows, grid_cols, grid_cols, grid_rows, depth_right
        )
        line = lax.dynamic_index_in_dim(right, col, 2, keepdims=False).transpose(2, 0, 1, 3)
        return left, line.reshape(grid_rows, -1)

    def wanted_by_row(labels):
        left, line = split_labels(labels)
        kept = labels[:, places_left + places_right :].reshape(
            grid_rows, grid_cols, rows_dev, retained_width
        )
        kept = lax.dynamic_index_in_dim(kept, col, 1, keepdims=False)
        inner_at = jnp.arange(KPB)
        keeps = flags(jnp.any(kept[:, :, :, None] == inner_at, axis=2))
        slot_a, col_a = split_label(left.transpose(2, 3, 0, 1, 4).reshape(grid_rows, grid_rows, -1))
        by_row = flags((slot_a // WA)[..., None] == jnp.arange(rows_dev))
        by_inner = flags(col_a[..., None] == inner_at)
        has = jnp.einsum("iker,ikeq->ikrq", by_row, by_inner, preferred_element_type=jnp.float32)
        uses = jnp.einsum(
            "ikrq,irj->kqij", has.astype(jnp.bfloat16), keeps, preferred_element_type=jnp.float32
        )
        slot_b, col_b = split_label(line)
        by_slot = flags((slot_b // WB)[..., None] == inner_at)
        found = jnp.einsum(
            "keq,kqij->keij", by_slot, flags(uses > 0.5), preferred_element_type=jnp.float32
        )
        found = jnp.sum(jnp.where(col_b[:, :, None, None] == inner_at, found, 0.0), axis=3)
        in_window = (rows_at[:, None] - rows_at[None, :] - col) % grid_rows < STEPS
        wanted = (found > 0.5) & in_window[:, None, :]
        wanted = wanted.transpose(2, 0, 1).reshape(grid_rows, -1)
        return jnp.stack([wanted, wanted[::-1]])

    def queues(places, capacity, arrived):
        into = jnp.stack(
            [
                lax.dynamic_index_in_dim(places[at], jnp.maximum(self_at[at] - 1, 0), 0, False)
                for at in range(2)
            ]
        )
        outof = jnp.stack(
            [
                lax.dynamic_index_in_dim(
                    places[at], jnp.minimum(self_at[at], grid_rows - 2), 0, False
                )
                for at in range(2)
            ]
        )
        come = jnp.stack(arrived(into))
        source = jnp.where(origins == self_at[:, None], place_home, come)
        hit = outof[:, None, :] == jnp.arange(capacity)[None, :, None]
        send = jnp.sum(jnp.where(hit, source[:, None, :], 0), axis=2)
        send = jnp.where((self_at < grid_rows - 1)[:, None], send, 0)
        lies = jnp.where(origins[0] <= row, source[0], come[1])
        return send, lies

    def products(lies, bounds, stage):
        left, line = split_labels(labels)
        slot_b, col_b = split_label(line)
        inner_at = jnp.arange(KPB)
        where_b = lies.reshape(grid_rows, -1)
        inner = (row + col + jnp.arange(STEPS)) % grid_rows
        slots = jnp.arange(slots_right)
        hit = jnp.take(slot_b, inner, axis=0)[:, None, :] == slots[:, None]
        b_at = jnp.sum(jnp.where(hit, jnp.take(where_b, inner, axis=0)[:, None, :], 0), axis=2)
        b_of = jnp.sum(jnp.where(hit, jnp.take(col_b, inner, axis=0)[:, None, :] + 1, 0), axis=2) - 1
        mine = lax.dynamic_index_in_dim(left, row, 2, keepdims=False)
        mine = jnp.take(mine, row ^ rows_at, axis=0)
        mine = jnp.take(mine, inner, axis=2).transpose(2, 1, 0, 3)
        slot_m, col_m = split_label(mine.reshape(STEPS, -1))
        base = jnp.arange(grid_cols)[:, None] * (places_left + 1)
        base = (base + rows_at * (grid_rows * depth_left)).reshape(1, -1, 1)
        a_place = base + inner[:, None, None] * depth_left + jnp.arange(depth_left)
        a_place = a_place.reshape(STEPS, -1)
        hit = slot_m[:, None, :] == jnp.arange(slots_left)[:, None]
        a_at = jnp.sum(jnp.where(hit, a_place[:, None, :], 0), axis=2)
        a_of = jnp.sum(jnp.where(hit, col_m[:, None, :] + 1, 0), axis=2) - 1
        meets = (a_of[:, :, None] == inner_at)[..., None]
        pair_at = jnp.sum(jnp.where(meets, b_at.reshape(STEPS, 1, KPB, WB), 0), axis=2)
        pair_of = jnp.sum(jnp.where(meets, b_of.reshape(STEPS, 1, KPB, WB) + 1, 0), axis=2) - 1
        kept = jnp.repeat(c_col, WA, axis=0)[None, :, None, :]
        same = (pair_of[..., None] == kept) & (kept >= 0)
        slot = jnp.sum(jnp.where(same, jnp.arange(retained_width) + 1, 0), axis=3) - 1
        target = (jnp.arange(slots_left) // WA)[None, :, None] * retained_width + slot
        left_code = (target * 2**23 + a_at[:, :, None] * 2**12).reshape(-1)
        valid = (slot >= 0).reshape(-1)
        pair_at = pair_at.reshape(-1)
        if bounds is None:
            return [compact(valid, left_code + pair_at)]
        down = pair_at >= local + capacity
        arrived = jnp.where(down, pair_at - capacity, pair_at) - local
        part, offset = locate(arrived, bounds)
        late = (part >= stage) & (arrived >= 0)
        rounds = len(bounds) - 1
        early_code = jnp.where(
            arrived < 0, pair_at, (part + 1 + jnp.where(down, stage, 0)) * 128 + offset
        )
        late_code = (part - stage + jnp.where(down, rounds - stage, 0)) * 128 + offset
        return [
            compact(valid & ~late, left_code + early_code),
            compact(valid & late, left_code + late_code),
        ]

    def plan(labels):
        places = queue_places(
            wanted_by_row(labels), origins, lambda place: available(place, ROUNDS, LAG)
        )
        send, lies = queues(
            places, capacity, lambda into: (local + into[0], local + capacity + into[1])
        )
        send = jnp.where(send >= local + capacity, send - capacity, send)
        part, offset = locate(send - local, starts)
        send = jnp.where(send < local, send, (part + 1) * 128 + offset)
        return send, lies, jnp.max(places) + 1

    send, lies, longest = one_turn(plan, hold(labels))
    longest = jnp.broadcast_to(longest.astype(jnp.float32), (1, edge, edge))
    home_right, send, longest, *home = lax.optimization_barrier((home_right, send, longest, *home))
    home_left = join([*home, longest])
    early, late = products(lies, starts, STAGE)
    left = lax.all_gather(home_left, "col", tiled=True)
    stride = home_left.shape[0]
    longest = jnp.max(left[stride - 1 :: stride, 0, 0]).astype(jnp.int32)
    kept_blocks = rows_dev * retained_width

    def send_round(at, ups, downs):
        seen = max(at - LAG + 1, 0)
        codes = send[:, int(starts[at]) : int(starts[at + 1])]
        go_up, go_down = pack_round(codes, home_right, ups[:seen], downs[:seen])
        return lax.ppermute(go_up, "row", up), lax.ppermute(go_down, "row", down)

    ups, downs = [], []
    for at in range(len(ROUNDS) - 1):
        came_up, came_down = send_round(at, ups, downs)
        ups.append(came_up)
        downs.append(came_down)
    total = multiply(*early, left, [home_right] + ups[:STAGE] + downs[:STAGE], kept_blocks)

    def finished(last_up, last_down):
        rights = [*ups[STAGE:], last_up, *downs[STAGE:], last_down]
        return multiply(*late, left, rights, kept_blocks, total)

    def usual():
        return finished(ups[-1], downs[-1])

    def longer():
        return finished(*send_round(len(ROUNDS) - 1, ups, downs))

    def looped():
        most = min((grid_rows - 1) * local, grid_rows * slots_right) + LOOP_ROUND * grid_rows
        most = -(-most // LOOP_ROUND) * LOOP_ROUND
        shared = most + LOOP_ROUND * (grid_rows + 1)
        end = local + shared
        places = queue_places(
            wanted_by_row(labels), origins, lambda place: (place // LOOP_ROUND + 1) * LOOP_ROUND
        )

        def from_end(place):
            return end - (place // LOOP_ROUND + 1) * LOOP_ROUND + place % LOOP_ROUND

        send, lies = queues(places, most, lambda into: (local + into[0], from_end(into[1])))
        rounds = (lax.pmax(jnp.max(places), ("row", "col")) + LOOP_ROUND) // LOOP_ROUND
        mine = [
            jnp.max(
                lax.dynamic_index_in_dim(places[at], jnp.maximum(self_at[at] - 1, 0), 0, False)
            )
            for at in range(2)
        ]
        mine = [jnp.where(self_at[at] > 0, mine[at], -1) for at in range(2)]
        ((codes, count),) = products(lies, None, None)
        store = jnp.zeros((end + LOOP_ROUND, edge, edge), jnp.float32)
        store = lax.dynamic_update_slice(store, home_right, (0, 0, 0))

        def one(at, store):
            index = lax.dynamic_slice(send, (0, at * LOOP_ROUND), (2, LOOP_ROUND))
            came = [
                lax.ppermute(jnp.take(store, index[side], axis=0, mode="clip"), "row", pairs)
                for side, pairs in ((0, up), (1, down))
            ]
            first = at * LOOP_ROUND
            for side, to in ((0, local + first), (1, end - first - LOOP_ROUND)):
                to = jnp.where(first <= mine[side], to, end)
                store = lax.dynamic_update_slice(store, came[side], (to, 0, 0))
            return store

        store = lax.fori_loop(0, rounds, one, store)
        return multiply(codes, count, left, [store], kept_blocks)

    usual_length = int(starts[-2])
    level = (longest > usual_length).astype(jnp.int32) + (longest > capacity).astype(jnp.int32)
    result = lax.switch(level, [usual, longer, looped])
    return result.reshape(rows_dev, retained_width, edge, edge)


def solution(mesh):
    return jax.shard_map(
        on_device,
        mesh=mesh,
        in_specs=(
            P(("row", "col"), None, None),
            P(("row", "col")),
            P(("row", "col")),
            P(("row", "col"), None, None),
            P(("row", "col")),
            P(("row", "col")),
            P("row", "col"),
        ),
        out_specs=P("row", "col", None, None),
        check_vma=False,
    )
```

time: 673 us -> 295 us (0.44); the launches traced: 661 us -> 292 us
  local copies, waits for them, and re-layouts: 179 us -> 17.4 us
  matrix products: 141 us -> 1.29 us
  starting transfers between devices: 166 us -> 39.6 us
  Pallas kernels: 0 us -> 75.7 us
  waiting for transfers between devices: 169 us -> 129 us
  between operations: 0.69 us -> 15.3 us
  other arithmetic: 3.77 us -> 12.4 us
    all_to_all x4 -> x2, waiting for transfers between devices: 168 us -> 3.95 us  [the longest x1 3.95 us: on_device(): lax.all_to_all(sent[-1], 'col', split_axis=0, concat_axis=0, tiled=True)]
    dot_general x13 -> x5, matrix products: 140 us -> 1.11 us  [the longest x2 0.47 us: compact(): jnp.dot(flags(valid)[None], before, preferred_element_type=jnp.float32)[0]]
    ppermute x8 -> x11, waiting for transfers between devices: 1.48 us -> 125 us  [the longest x8 97.4 us: send_round(): return (lax.ppermute(go_up, 'row', up), lax.ppermute(go_down, 'row', down))]
    ppermute x8 -> x11, starting transfers between devices: 146 us -> 28.6 us  [the longest x8 24.2 us: send_round(): return (lax.ppermute(go_up, 'row', up), lax.ppermute(go_down, 'row', down))]
    gather x12 -> x6, local copies, waits for them, and re-layouts: 87.9 us -> 3.38 us  [the longest x1 0.57 us: products(): mine = jnp.take(mine, row ^ rows_at, axis=0)]
    pallas_call x0 -> x9, Pallas kernels: none -> 75.7 us  [the longest x2 41.9 us: multiply(): pl.pallas_call(functools.partial(multiply_kernel, len(rights), first), ou...]
    transpose x3 -> x6, local copies, waits for them, and re-layouts: 59.4 us -> 0.7 us  [the longest x4 0.28 us: split_labels(): lax.dynamic_index_in_dim(right, col, 2, keepdims=False)]
    dot_general x4 -> x0, local copies, waits for them, and re-layouts: 15.1 us -> none  [the longest x2 8.8 us: pack_blocks(): jnp.dot(select, held_blocks.reshape(held_blocks.shape[0], -1), precision=...]
  transfers between devices with their start and end apart: 12 -> 14, of which waited for: 5 -> 9; matrix products, arithmetic and copies ran while one was open for 39% -> 8% of each run, Pallas kernels for 0% -> 22%
where the time goes in v1:
time: 295 us; the launch traced here: 292 us
  waiting for transfers between devices  129 us (44%)
  Pallas kernels  75.7 us (26%)
  starting transfers between devices  39.6 us (13%)
  local copies, waits for them, and re-layouts  17.4 us (6%)
  between operations  15.3 us (5%)
  other arithmetic  12.4 us (4%)
    ppermute x8, waiting for transfers between devices, send_round(): return (lax.ppermute(go_up, 'row', up), lax.ppermute(go_down, 'row', down))  97.4 us
    pallas_call x2, Pallas kernels, multiply(): pl.pallas_call(functools.partial(multiply_kernel, len(rights), first), ou...  41.9 us
    pallas_call x5, Pallas kernels, relay_call(): pl.pallas_call(kernel, out_shape=[jax.ShapeDtypeStruct((size,) + block, j...  30.8 us
    ppermute x3, waiting for transfers between devices, swap(): lax.ppermute(value, axis, [(at, at ^ distance) for at in range(count)])  28 us
    ppermute x8, starting transfers between devices, send_round(): return (lax.ppermute(go_up, 'row', up), lax.ppermute(go_down, 'row', down))  24.2 us
    all_to_all x1, starting transfers between devices, share(): lax.all_to_all(sent, ('row', 'col'), split_axis=0, concat_axis=0, tiled=T...  6.13 us
  transfers between devices with their start and end apart: 14, of which 9 were waited for; matrix products, arithmetic and copies ran while one was open for 8% of the time, Pallas kernels for 22%

profile of v1, /device:TPU:2, one launch (start us, length us, event | category | flops | bytes accessed | tf_op | source)
XLA Modules:
  0.0 292.2 jit_solution(13271192964682028676)
XLA Ops:
  10.1 6.1 %all-to-all-start = ((s32[32,1,192]{2,1,0:T(1,128)}), s32[32,1,192]{2,1,0:T(1,128)S(1)}, u32[]{:S(2)}, u32[]{:S(2)}) async-start(s32[32,1,192]{2,1,0:T(1,128)} %broadcast_in_dim.691), calls=%async_computation | async-start | bytes 65536 | tf_op jit(solution)/shard_map/all_to_all | solution.py:35
  17.8 6.6 %sort_blocks.1 = (f32[8,128,128]{2,1,0:T(8,128)}, f32[8,128,128]{2,1,0:T(8,128)}, f32[8,128,128]{2,1,0:T(8,128)}, f32[8,128,128]{2,1,0:T(8,128)}, f32[64,128,128]{2,1,0:T(8,128)}) custom-call(s32[96]{0:T(128)} %pad_add_fusion.3.index_ref, f32[32,128,128]{2,1,0:T(8,128)} %refs_0_.1, f32[64,128,128]{2,1,0:T(8,128)} %refs_1_.1), custom_call_target="tpu_custom_call" | custom-call | tf_op jit(solution)/shard_map/sort_blocks/pallas_call | solution.py:157
  24.5 4.8 %all-to-all-start.1 = ((f32[64,128,128]{2,1,0:T(8,128)}), f32[64,128,128]{2,1,0:T(8,128)}, u32[]{:S(2)}, u32[]{:S(2)}) async-start(f32[64,128,128]{2,1,0:T(8,128)} %get-tuple-element.548), calls=%async_computation.1 | async-start | bytes 8388608 | tf_op jit(solution)/shard_map/all_to_all | solution.py:400
  30.8 1.5 reduce_max.132
  32.8 1.8 collective-permute-start.4
  34.7 2.4 collective-permute-start.5
  38.5 6.6 %while.33 = (s32[]{:T(128)}, s32[2,120]{1,0:T(2,128)}, s32[256]{0:T(256)}, s32[]{:T(128)}, s32[]{:T(128)}, /*index=5*/s32[2]{0:T(128)S(1)}, s32[32,192]{0,1:T(8,...) while((s32[]{:T(128)}, s32[2,120]{1,0:T(2,128)}, ...), condition=%wide.region_15.16_spmd.clone.clone, body=%wide.region_7.15_spmd.sunk.clone.clone.sunk | while | flops 3601188 | bytes 610925 | solution.py:84
  45.1 12.6 %collective-permute-done.4.refs_1_ = f32[8,128,128]{2,1,0:T(8,128)S(1)} collective-permute-done((f32[8,128,128]{2,1,0:T(8,128)}, f32[8,128,128]{2,1,0:T(8,128)S(1)}, u32[]{:S(2)}, u32[]{:S(2)}) %collective-permute-start.4) | collective-permute-done | bytes 524320 | tf_op jit(solution)/shard_map/ppermute | solution.py:29
  57.7 15.4 %collective-permute-done.5.refs_2_ = f32[8,128,128]{2,1,0:T(8,128)S(1)} collective-permute-done((f32[8,128,128]{2,1,0:T(8,128)}, f32[8,128,128]{2,1,0:T(8,128)S(1)}, u32[]{:S(2)}, u32[]{:S(2)}) %collective-permute-start.5) | collective-permute-done | bytes 524320 | tf_op jit(solution)/shard_map/ppermute | solution.py:29
  73.1 3.9 %all-to-all-done.1.refs_0_ = f32[64,128,128]{2,1,0:T(8,128)} async-done(((f32[64,128,128]{2,1,0:T(8,128)}), f32[64,128,128]{2,1,0:T(8,128)}, u32[]{:S(2)}, u32[]{:S(2)}) %all-to-all-start.1) | async-done | bytes 4194336 | tf_op jit(solution)/shard_map/all_to_all | solution.py:400
  77.7 2.4 join.1
  80.8 5.4 %pack_round.6 = (f32[24,128,128]{2,1,0:T(8,128)}, f32[24,128,128]{2,1,0:T(8,128)}) custom-call(s32[48]{0:T(128)} %reshape.1602.index_ref, f32[64,128,128]{2,1,0:T(8,128)} %all-to-all-done.1.refs_0_), custom_call_target="tpu_custom_call" | custom-call | tf_op jit(solution)/shard_map/pack_round/pallas_call | solution.py:157
  86.2 8.1 %collective-permute-start.7 = (f32[24,128,128]{2,1,0:T(8,128)}, f32[24,128,128]{2,1,0:T(8,128)S(1)}, u32[]{:S(2)}, u32[]{:S(2)}) collective-permute-start(f32[24,128,128]{2,1,0:T(8,128)} %get-tuple-element.564), channel_id=1, source_target_pairs={{0,8},{8,16},{16,24},{1,9},{9,17},{17,25},{2,10},{10,18},{18,26},{... | collective-permute-start | bytes 4718600 | tf_op jit(solution)/shard_map/ppermute | solution.py:546
  94.3 1.3 collective-permute-start.8
  96.7 30.6 %collective-permute-done.7.refs_1_ = f32[24,128,128]{2,1,0:T(8,128)S(1)} collective-permute-done((f32[24,128,128]{2,1,0:T(8,128)}, f32[24,128,128]{2,1,0:T(8,128)S(1)}, u32[]{:S(2)}, u32[]{:S(2)}) %collective-permute-start.7) | collective-permute-done | bytes 1572896 | tf_op jit(solution)/shard_map/ppermute | solution.py:546
  127.3 4.1 %collective-permute-done.8.refs_2_.refs_3_.refs_4_ = f32[24,128,128]{2,1,0:T(8,128)S(1)} collective-permute-done((f32[24,128,128]{2,1,0:T(8,128)}, f32[24,128,128]{2,1,0:T(8,128)S(1)}, u32[]{:S(2)}, u32[]{:S(2)}) %collective-permute-start.8) | collective-permute-done | bytes 1572896 | tf_op jit(solution)/shard_map/ppermute | solution.py:546
  131.4 5.5 %pack_round.7 = (f32[24,128,128]{2,1,0:T(8,128)}, f32[24,128,128]{2,1,0:T(8,128)}) custom-call(s32[48]{0:T(128)} %reshape.1603.index_ref, f32[64,128,128]{2,1,0:T(8,128)} %all-to-all-done.1.refs_0_, f32[24,128,128]{2,1,0:T(8,128)S(1)} %collective-permute-done.7.refs_1_, f32[24,128,128]{2,1,0:T(8,128)S(1)} %collective-permute-done.8.refs_2_.refs_3_.refs_4_), custom_call_target="tpu_custom_call" | custom-call | tf_op jit(solution)/shard_map/pack_round/pallas_call | solution.py:157
  136.9 6.0 %collective-permute-start.9 = (f32[24,128,128]{2,1,0:T(8,128)}, f32[24,128,128]{2,1,0:T(8,128)}, u32[]{:S(2)}, u32[]{:S(2)}) collective-permute-start(f32[24,128,128]{2,1,0:T(8,128)} %get-tuple-element.566), channel_id=1, source_target_pairs={{0,8},{8,16},{16,24},{1,9},{9,17},{17,25},{2,10},{10,18},{18,26},{... | collective-permute-start | bytes 4718600 | tf_op jit(solution)/shard_map/ppermute | solution.py:546
  142.9 1.3 collective-permute-start.10
  149.4 24.8 %collective-permute-done.9.refs_2_ = f32[24,128,128]{2,1,0:T(8,128)} collective-permute-done((f32[24,128,128]{2,1,0:T(8,128)}, f32[24,128,128]{2,1,0:T(8,128)}, u32[]{:S(2)}, u32[]{:S(2)}) %collective-permute-start.9) | collective-permute-done | bytes 1572896 | tf_op jit(solution)/shard_map/ppermute | solution.py:546
  174.3 5.3 %collective-permute-done.10.refs_4_.refs_5_ = f32[24,128,128]{2,1,0:T(8,128)} collective-permute-done((f32[24,128,128]{2,1,0:T(8,128)}, f32[24,128,128]{2,1,0:T(8,128)}, u32[]{:S(2)}, u32[]{:S(2)}) %collective-permute-start.10) | collective-permute-done | bytes 1572896 | tf_op jit(solution)/shard_map/ppermute | solution.py:546
  179.5 6.7 %pack_round.8 = (f32[24,128,128]{2,1,0:T(8,128)}, f32[24,128,128]{2,1,0:T(8,128)}) custom-call(s32[48]{0:T(128)} %reshape.1604.index_ref, f32[64,128,128]{2,1,0:T(8,128)} %all-to-all-done.1.refs_0_, f32[24,128,128]{2,1,0:T(8,128)S(1)} %collective-permute-done.7.refs_1_, f32[24,128,128]{2,1,0:T(8,128)} %collective-permute-done.9.refs_2_, ...), custom_call_target="tpu_custom_call" | custom-call | tf_op jit(solution)/shard_map/pack_round/pallas_call | solution.py:157
  186.2 2.5 collective-permute-start.11
  191.8 27.3 %collective-permute-done.11.refs_3_ = f32[24,128,128]{2,1,0:T(8,128)} collective-permute-done((f32[24,128,128]{2,1,0:T(8,128)}, f32[24,128,128]{2,1,0:T(8,128)}, u32[]{:S(2)}, u32[]{:S(2)}) %collective-permute-start.11) | collective-permute-done | bytes 1572896 | tf_op jit(solution)/shard_map/ppermute | solution.py:546
  219.1 5.3 %collective-permute-done.12.refs_6_ = f32[24,128,128]{2,1,0:T(8,128)} collective-permute-done((f32[24,128,128]{2,1,0:T(8,128)}, f32[24,128,128]{2,1,0:T(8,128)}, u32[]{:S(2)}, u32[]{:S(2)}) %collective-permute-start.12) | collective-permute-done | bytes 1572896 | tf_op jit(solution)/shard_map/ppermute | solution.py:546
  224.4 6.7 %pack_round.9 = (f32[24,128,128]{2,1,0:T(8,128)}, f32[24,128,128]{2,1,0:T(8,128)}) custom-call(s32[48]{0:T(128)} %reshape.1601.index_ref, f32[64,128,128]{2,1,0:T(8,128)} %all-to-all-done.1.refs_0_, f32[24,128,128]{2,1,0:T(8,128)S(1)} %collective-permute-done.7.refs_1_, f32[24,128,128]{2,1,0:T(8,128)} %collective-permute-done.9.refs_2_, ...), custom_call_target="tpu_custom_call" | custom-call | tf_op jit(solution)/shard_map/pack_round/pallas_call | solution.py:157
  231.1 2.5 collective-permute-start.13
  238.4 1.4 slice_reduce_fusion.1
  240.5 32.4 %multiply.7 = f32[96,128,128]{2,1,0:T(8,128)} custom-call(s32[768]{0:T(1024)} %select_reduce_fusion.14.list_ref, s32[1]{0:T(128)} %bitcast.39.count_ref, f32[264,128,128]{2,1,0:T(8,128)} %all-gather.2.cloned.1.call-done.a_ref, f32[64,128,128]{2,1,0:T(8,128)} %all-to-all-done.1.refs_0_, f32[24,128,128]{2,1,0:T(8,128)S(1)} %collective-permute-done.7.refs_1_, ...), custom_call_target="tpu_custom_call" | custom-call | flops 1887436800 | bytes 67108864 | tf_op jit(solution)/shard_map/multiply/pallas_call | solution.py:324
  272.9 9.7 %conditional.1 = (f32[16,6,128,128]{3,2,1,0:T(8,128)S(1)}) conditional(s32[]{:T(128)} %clamp.3, (s32[768]{0:T(1024)S(1)}, s32[1]{0:T(128)}, f32[264,128,128]{2,1,0:T(8,128)}, f32[24,128,128]{2,1,0:T(8,128)}, f32[24,128,128]{2,1,0:T(8,128)}, /*index=5*/f32[96,128,128]{2,1,0:T(8,128)}) %tuple.60, (s32[2,120]{1,0:T(2,128)S(1)}, ...), branch_computations={%region_28.32_spmd, %region_29.33_spmd, %region_30.55_spmd} | conditional | flops 1895538944 | bytes 102508328 | solution.py:607
  272.9 9.5 %multiply.4 = f32[96,128,128]{2,1,0:T(8,128)S(1)} custom-call(s32[768]{0:T(1024)S(1)} %get-tuple-element.470.list_ref, s32[1]{0:T(128)} %get-tuple-element.471.count_ref, f32[264,128,128]{2,1,0:T(8,128)} %get-tuple-element.472.a_ref, f32[24,128,128]{2,1,0:T(8,128)} %get-tuple-element.473.refs_0_.refs_1_, f32[24,128,128]{2,1,0:T(8,128)} %get-tuple-element.473.refs_0_.refs_1_, ...), custom_call_target="tpu_custom_call" | custom-call | flops 1887436800 | bytes 67108864 | tf_op jit(solution)/shard_map/cond/branch_0_fun/multiply/pallas_call | solution.py:324
  282.6 2.7 copy-done
  (199 shorter events, 29.0 us)
Async XLA Ops:
  10.1 14.3 %all-to-all-start = ((s32[32,1,192]{2,1,0:T(1,128)}), s32[32,1,192]{2,1,0:T(1,128)S(1)}, u32[]{:S(2)}, u32[]{:S(2)}) async-start(s32[32,1,192]{2,1,0:T(1,128)} %broadcast_in_dim.691), calls=%async_computation | async-start | bytes 65536 | tf_op jit(solution)/shard_map/all_to_all | solution.py:35
  24.4 12.7 %copy-start.20 = (f32[8,128,128]{2,1,0:T(8,128)S(1)}, f32[8,128,128]{2,1,0:T(8,128)}, u32[]{:S(2)}) copy-start(f32[8,128,128]{2,1,0:T(8,128)} %get-tuple-element.555) | copy-start | bytes 1572868
  24.4 14.0 %copy-start.6 = (s32[2,256]{1,0:T(2,128)S(1)}, s32[2,256]{1,0:T(2,128)}, u32[]{:S(2)}) copy-start(s32[2,256]{1,0:T(2,128)} %constant.858.clone..sunk.3) | copy-start | bytes 6148
  24.4 14.0 %copy-start.7 = (s32[2,256]{1,0:T(2,128)S(1)}, s32[2,256]{1,0:T(2,128)}, u32[]{:S(2)}) copy-start(s32[2,256]{1,0:T(2,128)} %constant.1294) | copy-start | bytes 6148
  24.4 14.0 %copy-start.8 = (pred[2,1,256]{2,1,0:T(4,128)(4,1)S(1)}, pred[2,1,256]{2,1,0:T(4,128)(4,1)}, u32[]{:S(2)}) copy-start(pred[2,1,256]{2,1,0:T(4,128)(4,1)} %constant.1293) | copy-start | bytes 1540
  24.4 14.0 %copy-start.9 = (pred[2,1,256]{2,1,0:T(4,128)(4,1)S(1)}, pred[2,1,256]{2,1,0:T(4,128)(4,1)}, u32[]{:S(2)}) copy-start(pred[2,1,256]{2,1,0:T(4,128)(4,1)} %constant.1292) | copy-start | bytes 1540
  24.4 14.0 %copy-start.11 = (s32[256]{0:T(256)S(1)}, s32[256]{0:T(256)}, u32[]{:S(2)}) copy-start(s32[256]{0:T(256)} %constant.857.clone..sunk.3) | copy-start | bytes 3076
  24.5 14.0 %copy-start.12 = (s32[1,256]{1,0:T(1,128)S(1)}, s32[1,256]{1,0:T(1,128)}, u32[]{:S(2)}) copy-start(s32[1,256]{1,0:T(1,128)} %constant.1295) | copy-start | bytes 3076
  24.5 52.5 %all-to-all-start.1 = ((f32[64,128,128]{2,1,0:T(8,128)}), f32[64,128,128]{2,1,0:T(8,128)}, u32[]{:S(2)}, u32[]{:S(2)}) async-start(f32[64,128,128]{2,1,0:T(8,128)} %get-tuple-element.548), calls=%async_computation.1 | async-start | bytes 8388608 | tf_op jit(solution)/shard_map/all_to_all | solution.py:400
  29.3 209.1 %all-gather.2.cloned.1.call-start = ((), (), s32[]{:S(2)}) async-start(), calls=%async_computation.2 | async-start | bytes 19464192 | tf_op jit(solution)/shard_map/all_gather | solution.py:537
  32.8 24.9 %collective-permute-start.4 = (f32[8,128,128]{2,1,0:T(8,128)}, f32[8,128,128]{2,1,0:T(8,128)S(1)}, u32[]{:S(2)}, u32[]{:S(2)}) collective-permute-start(f32[8,128,128]{2,1,0:T(8,128)} %get-tuple-element.553), channel_id=1, source_target_pairs={{0,8},{8,0},{16,24},{24,16},{1,9},{9,1},{17,25},{25,17},{2,10},{10... | collective-permute-start | bytes 1572872 | tf_op jit(solution)/shard_map/ppermute | solution.py:29
  34.7 38.4 %collective-permute-start.5 = (f32[8,128,128]{2,1,0:T(8,128)}, f32[8,128,128]{2,1,0:T(8,128)S(1)}, u32[]{:S(2)}, u32[]{:S(2)}) collective-permute-start(f32[8,128,128]{2,1,0:T(8,128)} %get-tuple-element.554), channel_id=1, source_target_pairs={{0,16},{8,24},{16,0},{24,8},{1,17},{9,25},{17,1},{25,9},{2,18},{10... | collective-permute-start | bytes 1572872 | tf_op jit(solution)/shard_map/ppermute | solution.py:29
  37.1 36.0 %collective-permute-start.6 = (f32[8,128,128]{2,1,0:T(8,128)S(1)}, f32[8,128,128]{2,1,0:T(8,128)S(1)}, u32[]{:S(2)}, u32[]{:S(2)}) collective-permute-start(f32[8,128,128]{2,1,0:T(8,128)S(1)} %copy-done.20), channel_id=1, source_target_pairs={{0,24},{8,16},{16,8},{24,0},{1,25},{9,17},{17,9},{25,1},{2,26},{10... | collective-permute-start | bytes 1572872 | tf_op jit(solution)/shard_map/ppermute | solution.py:29
  57.7 19.9 %copy-start.3 = (f32[8,128,128]{2,1,0:T(8,128)}, f32[8,128,128]{2,1,0:T(8,128)S(1)}, u32[]{:S(2)}) copy-start(f32[8,128,128]{2,1,0:T(8,128)S(1)} %collective-permute-done.4.refs_1_) | copy-start | bytes 1572868
  73.1 4.6 %copy-start.4 = (f32[8,128,128]{2,1,0:T(8,128)}, f32[8,128,128]{2,1,0:T(8,128)S(1)}, u32[]{:S(2)}) copy-start(f32[8,128,128]{2,1,0:T(8,128)S(1)} %collective-permute-done.5.refs_2_) | copy-start | bytes 1572868
  73.1 4.6 %copy-start.5 = (f32[8,128,128]{2,1,0:T(8,128)}, f32[8,128,128]{2,1,0:T(8,128)S(1)}, u32[]{:S(2)}) copy-start(f32[8,128,128]{2,1,0:T(8,128)S(1)} %collective-permute-done.6.refs_3_) | copy-start | bytes 1572868
  77.7 2.5 copy-start.13
  86.2 41.1 %collective-permute-start.7 = (f32[24,128,128]{2,1,0:T(8,128)}, f32[24,128,128]{2,1,0:T(8,128)S(1)}, u32[]{:S(2)}, u32[]{:S(2)}) collective-permute-start(f32[24,128,128]{2,1,0:T(8,128)} %get-tuple-element.564), channel_id=1, source_target_pairs={{0,8},{8,16},{16,24},{1,9},{9,17},{17,25},{2,10},{10,18},{18,26},{... | collective-permute-start | bytes 4718600 | tf_op jit(solution)/shard_map/ppermute | solution.py:546
  94.3 37.1 %collective-permute-start.8 = (f32[24,128,128]{2,1,0:T(8,128)}, f32[24,128,128]{2,1,0:T(8,128)S(1)}, u32[]{:S(2)}, u32[]{:S(2)}) collective-permute-start(f32[24,128,128]{2,1,0:T(8,128)} %get-tuple-element.565), channel_id=1, source_target_pairs={{8,0},{16,8},{24,16},{9,1},{17,9},{25,17},{10,2},{18,10},{26,18},{... | collective-permute-start | bytes 4718600 | tf_op jit(solution)/shard_map/ppermute | solution.py:546
  96.6 47.7 %copy-start.10 = (s32[16,6]{0,1:T(8,128)S(1)}, s32[16,6]{0,1:T(8,128)}, u32[]{:S(2)}) copy-start(s32[16,6]{0,1:T(8,128)} %param.28) | copy-start | bytes 1156
  96.7 49.9 %copy-start.18 = (s32[256]{0:T(256)S(1)}, s32[256]{0:T(256)}, u32[]{:S(2)}) copy-start(s32[256]{0:T(256)} %get-tuple-element.561) | copy-start | bytes 3076
  136.9 37.3 %collective-permute-start.9 = (f32[24,128,128]{2,1,0:T(8,128)}, f32[24,128,128]{2,1,0:T(8,128)}, u32[]{:S(2)}, u32[]{:S(2)}) collective-permute-start(f32[24,128,128]{2,1,0:T(8,128)} %get-tuple-element.566), channel_id=1, source_target_pairs={{0,8},{8,16},{16,24},{1,9},{9,17},{17,25},{2,10},{10,18},{18,26},{... | collective-permute-start | bytes 4718600 | tf_op jit(solution)/shard_map/ppermute | solution.py:546
  142.9 36.6 %collective-permute-start.10 = (f32[24,128,128]{2,1,0:T(8,128)}, f32[24,128,128]{2,1,0:T(8,128)}, u32[]{:S(2)}, u32[]{:S(2)}) collective-permute-start(f32[24,128,128]{2,1,0:T(8,128)} %get-tuple-element.567), channel_id=1, source_target_pairs={{8,0},{16,8},{24,16},{9,1},{17,9},{25,17},{10,2},{18,10},{26,18},{... | collective-permute-start | bytes 4718600 | tf_op jit(solution)/shard_map/ppermute | solution.py:546
  186.2 32.9 %collective-permute-start.11 = (f32[24,128,128]{2,1,0:T(8,128)}, f32[24,128,128]{2,1,0:T(8,128)}, u32[]{:S(2)}, u32[]{:S(2)}) collective-permute-start(f32[24,128,128]{2,1,0:T(8,128)} %get-tuple-element.568), channel_id=1, source_target_pairs={{0,8},{8,16},{16,24},{1,9},{9,17},{17,25},{2,10},{10,18},{18,26},{... | collective-permute-start | bytes 4718600 | tf_op jit(solution)/shard_map/ppermute | solution.py:546
  188.7 35.7 %collective-permute-start.12 = (f32[24,128,128]{2,1,0:T(8,128)}, f32[24,128,128]{2,1,0:T(8,128)}, u32[]{:S(2)}, u32[]{:S(2)}) collective-permute-start(f32[24,128,128]{2,1,0:T(8,128)} %get-tuple-element.569), channel_id=1, source_target_pairs={{8,0},{16,8},{24,16},{9,1},{17,9},{25,17},{10,2},{18,10},{26,18},{... | collective-permute-start | bytes 4718600 | tf_op jit(solution)/shard_map/ppermute | solution.py:546
  231.1 41.8 %collective-permute-start.13 = (f32[24,128,128]{2,1,0:T(8,128)}, f32[24,128,128]{2,1,0:T(8,128)}, u32[]{:S(2)}, u32[]{:S(2)}) collective-permute-start(f32[24,128,128]{2,1,0:T(8,128)} %get-tuple-element.570), channel_id=1, source_target_pairs={{0,8},{8,16},{16,24},{1,9},{9,17},{17,25},{2,10},{10,18},{18,26},{... | collective-permute-start | bytes 4718600 | tf_op jit(solution)/shard_map/ppermute | solution.py:546
  233.6 39.3 %collective-permute-start.14 = (f32[24,128,128]{2,1,0:T(8,128)}, f32[24,128,128]{2,1,0:T(8,128)}, u32[]{:S(2)}, u32[]{:S(2)}) collective-permute-start(f32[24,128,128]{2,1,0:T(8,128)} %get-tuple-element.571), channel_id=1, source_target_pairs={{8,0},{16,8},{24,16},{9,1},{17,9},{25,17},{10,2},{18,10},{26,18},{... | collective-permute-start | bytes 4718600 | tf_op jit(solution)/shard_map/ppermute | solution.py:546
  282.6 2.7 copy-start
Sparse Core Ops, SparseCore 0:
  80.2 97.5 all-gather.1

commit v2 on v1

--- a/solution.py
+++ b/solution.py
@@ -13,12 +13,14 @@
 WB = 4
 STEPS = 3
 LABEL = 32
-ROUNDS = (24,) * 5
-LAG = 1
-STAGE = 3
+ROUNDS = (12,) * 8 + (24,)
+LAG = 2
+STAGE = 7
 FAR = 1 << 16
 LOOP_ROUND = 8
-SLOTS = 8
+SLOTS = 32
+GROUP = 8
+WEIGHT = 100
 VMEM_BYTES = 56 * 2**20
 
 
@@ -150,7 +152,7 @@
         pltpu.make_async_copy(out, out, store_sem).wait()
 
 
-def relay_call(kernel, name, codes, sources, sizes):
+def relay_call(kernel, name, codes, sources, sizes, weight=0):
     block = sources[0].shape[1:]
     total = sum(sizes)
     hbm = pl.BlockSpec(memory_space=pltpu.HBM)
@@ -165,7 +167,7 @@
             pltpu.SemaphoreType.DMA,
         ],
         compiler_params=local_params(),
-        cost_estimate=copy_costs(0, block[0]),
+        cost_estimate=copy_costs(weight, block[0]),
         name=name,
     )(codes, *sources)
 
@@ -252,10 +254,10 @@
     relay(load, outs, buf, load_sem, store_sem)
 
 
-def pack_round(codes, own, ups, downs):
+def pack_round(codes, own, ups, downs, weight):
     size = codes.shape[1]
     kernel = functools.partial(pack_kernel, len(ups), size)
-    return relay_call(kernel, "pack_round", codes.reshape(-1), [own, *ups, *downs], [size, size])
+    return relay_call(kernel, "pack_round", codes.reshape(-1), [own, *ups, *downs], [size, size], weight)
 
 
 def multiply_kernel(rights, first, list_ref, count_ref, a_ref, *refs):
@@ -289,28 +291,40 @@
 
         lax.fori_loop(0, kept, clear, 0)
     else:
-        load = pltpu.make_async_copy(c_ref, acc, c_sem)
+        load = pltpu.make_async_copy(c_ref, acc.at[pl.ds(0, kept)], c_sem)
         load.start()
         load.wait()
 
-    def step(at, carry):
-        slot = lax.rem(at, SLOTS)
-        pltpu.make_async_copy(a_buf.at[slot], a_buf.at[slot], a_sem.at[slot]).wait()
-        pltpu.make_async_copy(b_buf.at[slot], b_buf.at[slot], b_sem.at[slot]).wait()
-        a = a_buf[slot]
-        b = b_buf[slot]
-        a_hi = a.astype(jnp.bfloat16)
-        b_hi = b.astype(jnp.bfloat16)
-        a_lo = (a - a_hi.astype(jnp.float32)).astype(jnp.bfloat16)
-        b_lo = (b - b_hi.astype(jnp.float32)).astype(jnp.bfloat16)
-        dot = functools.partial(jnp.dot, preferred_element_type=jnp.float32)
-        target = lax.shift_right_logical(list_ref[at], 23)
-        acc[target] += dot(a_hi, b_hi) + (dot(a_hi, b_lo) + dot(a_lo, b_hi))
-        fetch(at + SLOTS)
+    def step(group, carry):
+        first_at = group * GROUP
+        for at in range(GROUP):
+            slot = lax.rem(first_at + at, SLOTS)
+            pltpu.make_async_copy(a_buf.at[slot], a_buf.at[slot], a_sem.at[slot]).wait()
+            pltpu.make_async_copy(b_buf.at[slot], b_buf.at[slot], b_sem.at[slot]).wait()
+        results = []
+        for at in range(GROUP):
+            slot = lax.rem(first_at + at, SLOTS)
+            a = a_buf[slot]
+            b = b_buf[slot]
+            a_hi = a.astype(jnp.bfloat16)
+            b_hi = b.astype(jnp.bfloat16)
+            a_lo = (a - a_hi.astype(jnp.float32)).astype(jnp.bfloat16)
+            b_lo = (b - b_hi.astype(jnp.float32)).astype(jnp.bfloat16)
+            results.append(
+                jnp.dot(
+                    jnp.concatenate([a_hi, a_lo, a_hi], axis=1),
+                    jnp.concatenate([b_hi, b_hi, b_lo], axis=0),
+                    preferred_element_type=jnp.float32,
+                )
+            )
+        for at in range(GROUP):
+            acc[lax.shift_right_logical(list_ref[first_at + at], 23)] += results[at]
+        for at in range(GROUP):
+            fetch(first_at + at + SLOTS)
         return carry
 
-    lax.fori_loop(0, count, step, 0)
-    store = pltpu.make_async_copy(acc, out_ref, c_sem)
+    lax.fori_loop(0, count // GROUP, step, 0)
+    store = pltpu.make_async_copy(acc.at[pl.ds(0, kept)], out_ref, c_sem)
     store.start()
     store.wait()
 
@@ -327,7 +341,7 @@
         in_specs=[smem, smem] + [hbm] * len(arrays),
         out_specs=hbm,
         scratch_shapes=[
-            pltpu.VMEM((kept,) + block, jnp.float32),
+            pltpu.VMEM((kept + 1,) + block, jnp.float32),
             pltpu.VMEM((SLOTS,) + block, jnp.float32),
             pltpu.VMEM((SLOTS,) + block, jnp.float32),
             pltpu.SemaphoreType.DMA((SLOTS,)),
@@ -355,14 +369,16 @@
     )(values)
 
 
-def compact(valid, codes):
+def compact(valid, codes, spare):
     candidates = valid.shape[0]
     position = jnp.arange(candidates)
     before = flags(position[:, None] < position[None, :])
     place = jnp.dot(flags(valid)[None], before, preferred_element_type=jnp.float32)[0]
-    hit = (place.astype(jnp.int32)[None, :] == position[:, None]) & valid[None, :]
-    packed = jnp.sum(jnp.where(hit, codes[None, :], 0), axis=1)
-    return packed, jnp.sum(valid.astype(jnp.int32)).reshape(1)
+    listed = jnp.arange(-(-candidates // GROUP) * GROUP)
+    hit = (place.astype(jnp.int32)[None, :] == listed[:, None]) & valid[None, :]
+    packed = jnp.sum(jnp.where(hit, codes[None, :] - spare, 0), axis=1) + spare
+    count = jnp.sum(valid.astype(jnp.int32))
+    return packed, ((count + GROUP - 1) // GROUP * GROUP).reshape(1)
 
 
 def on_device(a_held, a_slot, a_col, b_held, b_slot, b_col, c_col):
@@ -499,10 +515,11 @@
         slot = jnp.sum(jnp.where(same, jnp.arange(retained_width) + 1, 0), axis=3) - 1
         target = (jnp.arange(slots_left) // WA)[None, :, None] * retained_width + slot
         left_code = (target * 2**23 + a_at[:, :, None] * 2**12).reshape(-1)
+        spare = rows_dev * retained_width * 2**23
         valid = (slot >= 0).reshape(-1)
         pair_at = pair_at.reshape(-1)
         if bounds is None:
-            return [compact(valid, left_code + pair_at)]
+            return [compact(valid, left_code + pair_at, spare)]
         down = pair_at >= local + capacity
         arrived = jnp.where(down, pair_at - capacity, pair_at) - local
         part, offset = locate(arrived, bounds)
@@ -513,8 +530,8 @@
         )
         late_code = (part - stage + jnp.where(down, rounds - stage, 0)) * 128 + offset
         return [
-            compact(valid & ~late, left_code + early_code),
-            compact(valid & late, left_code + late_code),
+            compact(valid & ~late, left_code + early_code, spare),
+            compact(valid & late, left_code + late_code, spare),
         ]
 
     def plan(labels):
@@ -542,7 +559,7 @@
     def send_round(at, ups, downs):
         seen = max(at - LAG + 1, 0)
         codes = send[:, int(starts[at]) : int(starts[at + 1])]
-        go_up, go_down = pack_round(codes, home_right, ups[:seen], downs[:seen])
+        go_up, go_down = pack_round(codes, home_right, ups[:seen], downs[:seen], WEIGHT * (at == 1))
         return lax.ppermute(go_up, "row", up), lax.ppermute(go_down, "row", down)
 
     ups, downs = [], []

time: 295 us -> 260 us (0.88)
  waiting for transfers between devices: 129 us -> 74.7 us
  starting transfers between devices: 39.6 us -> 62.1 us
  Pallas kernels: 75.7 us -> 69.4 us
    ppermute x8 -> x16, waiting for transfers between devices: 97.4 us -> 42.7 us  [send_round(): return (lax.ppermute(go_up, 'row', up), lax.ppermute(go_down, 'row', down))]
    ppermute x8 -> x16, starting transfers between devices: 24.2 us -> 46.7 us  [send_round(): return (lax.ppermute(go_up, 'row', up), lax.ppermute(go_down, 'row', down))]
    pallas_call x2, Pallas kernels: 41.9 us -> 28.1 us  [multiply(): pl.pallas_call(functools.partial(multiply_kernel, len(rights), first), ou...]
    pallas_call x5 -> x9, Pallas kernels: 30.8 us -> 38.4 us  [relay_call(): pl.pallas_call(kernel, out_shape=[jax.ShapeDtypeStruct((size,) + block, j...]
  transfers between devices with their start and end apart: 14 -> 22, of which waited for: 9 -> 16; matrix products, arithmetic and copies ran while one was open for 8% -> 10% of each run, Pallas kernels for 22% -> 24%
where the time goes in v2:
time: 260 us; the launch traced here: 258 us
  waiting for transfers between devices  74.7 us (29%)
  Pallas kernels  69.4 us (27%)
  starting transfers between devices  62.1 us (24%)
  local copies, waits for them, and re-layouts  20 us (8%)
  between operations  16.6 us (6%)
  other arithmetic  12.5 us (5%)
    ppermute x16, starting transfers between devices, send_round(): return (lax.ppermute(go_up, 'row', up), lax.ppermute(go_down, 'row', down))  46.7 us
    ppermute x16, waiting for transfers between devices, send_round(): return (lax.ppermute(go_up, 'row', up), lax.ppermute(go_down, 'row', down))  42.7 us
    pallas_call x9, Pallas kernels, relay_call(): pl.pallas_call(kernel, out_shape=[jax.ShapeDtypeStruct((size,) + block, j...  38.4 us
    pallas_call x2, Pallas kernels, multiply(): pl.pallas_call(functools.partial(multiply_kernel, len(rights), first), ou...  28.1 us
    ppermute x3, waiting for transfers between devices, swap(): lax.ppermute(value, axis, [(at, at ^ distance) for at in range(count)])  27.9 us
    all_to_all x1, starting transfers between devices, share(): lax.all_to_all(sent, ('row', 'col'), split_axis=0, concat_axis=0, tiled=T...  6.13 us
  transfers between devices with their start and end apart: 22, of which 16 were waited for; matrix products, arithmetic and copies ran while one was open for 10% of the time, Pallas kernels for 24%

profile of v2, /device:TPU:2, one launch (start us, length us, event | category | flops | bytes accessed | tf_op | source)
XLA Modules:
  0.0 257.7 jit_solution(9356344416395911405)
XLA Ops:
  10.1 6.1 %all-to-all-start = ((s32[32,1,192]{2,1,0:T(1,128)}), s32[32,1,192]{2,1,0:T(1,128)S(1)}, u32[]{:S(2)}, u32[]{:S(2)}) async-start(s32[32,1,192]{2,1,0:T(1,128)} %broadcast_in_dim.719), calls=%async_computation | async-start | bytes 65536 | tf_op jit(solution)/shard_map/all_to_all | solution.py:37
  17.8 6.6 %sort_blocks.1 = (f32[8,128,128]{2,1,0:T(8,128)}, f32[8,128,128]{2,1,0:T(8,128)}, f32[8,128,128]{2,1,0:T(8,128)}, f32[8,128,128]{2,1,0:T(8,128)}, f32[64,128,128]{2,1,0:T(8,128)}) custom-call(s32[96]{0:T(128)} %pad_add_fusion.3.index_ref, f32[32,128,128]{2,1,0:T(8,128)} %refs_0_.1, f32[64,128,128]{2,1,0:T(8,128)} %refs_1_.1), custom_call_target="tpu_custom_call" | custom-call | tf_op jit(solution)/shard_map/sort_blocks/pallas_call | solution.py:159
  24.5 4.8 %all-to-all-start.1 = ((f32[64,128,128]{2,1,0:T(8,128)}), f32[64,128,128]{2,1,0:T(8,128)}, u32[]{:S(2)}, u32[]{:S(2)}) async-start(f32[64,128,128]{2,1,0:T(8,128)} %get-tuple-element.580), calls=%async_computation.1 | async-start | bytes 8388608 | tf_op jit(solution)/shard_map/all_to_all | solution.py:416
  38.5 6.7 %while.33 = (s32[]{:T(128)}, s32[2,120]{1,0:T(2,128)}, s32[256]{0:T(256)}, s32[]{:T(128)}, s32[]{:T(128)}, /*index=5*/s32[2]{0:T(128)S(1)}, s32[32,192]{0,1:T(8,...) while((s32[]{:T(128)}, s32[2,120]{1,0:T(2,128)}, ...), condition=%wide.region_15.16_spmd.clone.clone, body=%wide.region_7.15_spmd.sunk.clone.clone.sunk | while | flops 3615204 | bytes 610925 | solution.py:86
  45.1 12.6 %collective-permute-done.4.refs_1_ = f32[8,128,128]{2,1,0:T(8,128)S(1)} collective-permute-done((f32[8,128,128]{2,1,0:T(8,128)}, f32[8,128,128]{2,1,0:T(8,128)S(1)}, u32[]{:S(2)}, u32[]{:S(2)}) %collective-permute-start.4) | collective-permute-done | bytes 524320 | tf_op jit(solution)/shard_map/ppermute | solution.py:31
  57.7 15.4 %collective-permute-done.5.refs_2_ = f32[8,128,128]{2,1,0:T(8,128)S(1)} collective-permute-done((f32[8,128,128]{2,1,0:T(8,128)}, f32[8,128,128]{2,1,0:T(8,128)S(1)}, u32[]{:S(2)}, u32[]{:S(2)}) %collective-permute-start.5) | collective-permute-done | bytes 524320 | tf_op jit(solution)/shard_map/ppermute | solution.py:31
  73.1 3.9 %all-to-all-done.1.refs_0_ = f32[64,128,128]{2,1,0:T(8,128)} async-done(((f32[64,128,128]{2,1,0:T(8,128)}), f32[64,128,128]{2,1,0:T(8,128)}, u32[]{:S(2)}, u32[]{:S(2)}) %all-to-all-start.1) | async-done | bytes 4194336 | tf_op jit(solution)/shard_map/all_to_all | solution.py:416
  84.1 3.7 %pack_round.10 = (f32[12,128,128]{2,1,0:T(8,128)}, f32[12,128,128]{2,1,0:T(8,128)}) custom-call(s32[24]{0:T(128)} %reshape.1688.index_ref, f32[64,128,128]{2,1,0:T(8,128)} %all-to-all-done.1.refs_0_), custom_call_target="tpu_custom_call" | custom-call | tf_op jit(solution)/shard_map/pack_round/pallas_call | solution.py:159
  87.7 8.2 %collective-permute-start.7 = (f32[12,128,128]{2,1,0:T(8,128)}, f32[12,128,128]{2,1,0:T(8,128)S(1)}, u32[]{:S(2)}, u32[]{:S(2)}) collective-permute-start(f32[12,128,128]{2,1,0:T(8,128)} %get-tuple-element.596), channel_id=1, source_target_pairs={{0,8},{8,16},{16,24},{1,9},{9,17},{17,25},{2,10},{10,18},{18,26},{... | collective-permute-start | bytes 2359304 | tf_op jit(solution)/shard_map/ppermute | solution.py:563
  98.1 3.6 %pack_round.11 = (f32[12,128,128]{2,1,0:T(8,128)}, f32[12,128,128]{2,1,0:T(8,128)}) custom-call(s32[24]{0:T(128)} %reshape.1689.index_ref, f32[64,128,128]{2,1,0:T(8,128)} %all-to-all-done.1.refs_0_), custom_call_target="tpu_custom_call" | custom-call | bytes 13107200 | tf_op jit(solution)/shard_map/pack_round/pallas_call | solution.py:159
  101.7 4.0 %collective-permute-start.8 = (f32[12,128,128]{2,1,0:T(8,128)}, f32[12,128,128]{2,1,0:T(8,128)S(1)}, u32[]{:S(2)}, u32[]{:S(2)}) collective-permute-start(f32[12,128,128]{2,1,0:T(8,128)} %get-tuple-element.597), channel_id=1, source_target_pairs={{0,8},{8,16},{16,24},{1,9},{9,17},{17,25},{2,10},{10,18},{18,26},{... | collective-permute-start | bytes 2359304 | tf_op jit(solution)/shard_map/ppermute | solution.py:563
  109.5 4.8 %collective-permute-done.7.refs_1_ = f32[12,128,128]{2,1,0:T(8,128)S(1)} collective-permute-done((f32[12,128,128]{2,1,0:T(8,128)}, f32[12,128,128]{2,1,0:T(8,128)S(1)}, u32[]{:S(2)}, u32[]{:S(2)}) %collective-permute-start.7) | collective-permute-done | bytes 786464 | tf_op jit(solution)/shard_map/ppermute | solution.py:563
  114.2 4.3 %collective-permute-done.9.refs_2_.refs_3_.refs_4_.refs_5_.refs_7_.refs_6_.refs_8_ = f32[12,128,128]{2,1,0:T(8,128)S(1)} collective-permute-done((f32[12,128,128]{2,1,0:T(8,128)}, f32[12,128,128]{2,1,0:T(8,128)S(1)}, u32[]{:S(2)}, u32[]{:S(2)}) %collective-permute-start.9) | collective-permute-done | bytes 786464 | tf_op jit(solution)/shard_map/ppermute | solution.py:563
  118.6 3.7 %pack_round.12 = (f32[12,128,128]{2,1,0:T(8,128)}, f32[12,128,128]{2,1,0:T(8,128)}) custom-call(s32[24]{0:T(128)} %reshape.1690.index_ref, f32[64,128,128]{2,1,0:T(8,128)} %all-to-all-done.1.refs_0_, f32[12,128,128]{2,1,0:T(8,128)S(1)} %collective-permute-done.7.refs_1_, ...), custom_call_target="tpu_custom_call" | custom-call | tf_op jit(solution)/shard_map/pack_round/pallas_call | solution.py:159
  122.3 5.0 %collective-permute-start.10 = (f32[12,128,128]{2,1,0:T(8,128)}, f32[12,128,128]{2,1,0:T(8,128)}, u32[]{:S(2)}, u32[]{:S(2)}) collective-permute-start(f32[12,128,128]{2,1,0:T(8,128)} %get-tuple-element.599), channel_id=1, source_target_pairs={{0,8},{8,16},{16,24},{1,9},{9,17},{17,25},{2,10},{10,18},{18,26},{... | collective-permute-start | bytes 2359304 | tf_op jit(solution)/shard_map/ppermute | solution.py:563
  131.1 4.3 %collective-permute-done.11.refs_4_.refs_5_.refs_6_.refs_8_.refs_7_.refs_9_ = f32[12,128,128]{2,1,0:T(8,128)S(1)} collective-permute-done((f32[12,128,128]{2,1,0:T(8,128)}, f32[12,128,128]{2,1,0:T(8,128)S(1)}, u32[]{:S(2)}, u32[]{:S(2)}) %collective-permute-start.11) | collective-permute-done | bytes 786464 | tf_op jit(solution)/shard_map/ppermute | solution.py:563
  135.4 3.7 %pack_round.13 = (f32[12,128,128]{2,1,0:T(8,128)}, f32[12,128,128]{2,1,0:T(8,128)}) custom-call(s32[24]{0:T(128)} %reshape.1691.index_ref, f32[64,128,128]{2,1,0:T(8,128)} %all-to-all-done.1.refs_0_, f32[12,128,128]{2,1,0:T(8,128)S(1)} %collective-permute-done.7.refs_1_, f32[12,128,128]{2,1,0:T(8,128)S(1)} %collective-permute-done.8.refs_2_, ...), custom_call_target="tpu_custom_call" | custom-call | tf_op jit(solution)/shard_map/pack_round/pallas_call | solution.py:159
  139.2 5.2 %collective-permute-start.12 = (f32[12,128,128]{2,1,0:T(8,128)}, f32[12,128,128]{2,1,0:T(8,128)}, u32[]{:S(2)}, u32[]{:S(2)}) collective-permute-start(f32[12,128,128]{2,1,0:T(8,128)} %get-tuple-element.601), channel_id=1, source_target_pairs={{0,8},{8,16},{16,24},{1,9},{9,17},{17,25},{2,10},{10,18},{18,26},{... | collective-permute-start | bytes 2359304 | tf_op jit(solution)/shard_map/ppermute | solution.py:563
  147.9 4.4 %collective-permute-done.13.refs_6_.refs_7_.refs_9_.refs_8_.refs_10_ = f32[12,128,128]{2,1,0:T(8,128)} collective-permute-done((f32[12,128,128]{2,1,0:T(8,128)}, f32[12,128,128]{2,1,0:T(8,128)}, u32[]{:S(2)}, u32[]{:S(2)}) %collective-permute-start.13) | collective-permute-done | bytes 786464 | tf_op jit(solution)/shard_map/ppermute | solution.py:563
  152.4 4.2 %pack_round.14 = (f32[12,128,128]{2,1,0:T(8,128)}, f32[12,128,128]{2,1,0:T(8,128)}) custom-call(s32[24]{0:T(128)} %reshape.1692.index_ref, f32[64,128,128]{2,1,0:T(8,128)} %all-to-all-done.1.refs_0_, f32[12,128,128]{2,1,0:T(8,128)S(1)} %collective-permute-done.7.refs_1_, f32[12,128,128]{2,1,0:T(8,128)S(1)} %collective-permute-done.8.refs_2_, ...), custom_call_target="tpu_custom_call" | custom-call | tf_op jit(solution)/shard_map/pack_round/pallas_call | solution.py:159
  156.6 3.2 %collective-permute-start.14 = (f32[12,128,128]{2,1,0:T(8,128)}, f32[12,128,128]{2,1,0:T(8,128)}, u32[]{:S(2)}, u32[]{:S(2)}) collective-permute-start(f32[12,128,128]{2,1,0:T(8,128)} %get-tuple-element.603), channel_id=1, source_target_pairs={{0,8},{8,16},{16,24},{1,9},{9,17},{17,25},{2,10},{10,18},{18,26},{... | collective-permute-start | bytes 2359304 | tf_op jit(solution)/shard_map/ppermute | solution.py:563
  164.8 4.4 %collective-permute-done.15.refs_8_.refs_10_.refs_9_.refs_11_ = f32[12,128,128]{2,1,0:T(8,128)} collective-permute-done((f32[12,128,128]{2,1,0:T(8,128)}, f32[12,128,128]{2,1,0:T(8,128)}, u32[]{:S(2)}, u32[]{:S(2)}) %collective-permute-start.15) | collective-permute-done | bytes 786464 | tf_op jit(solution)/shard_map/ppermute | solution.py:563
  169.2 4.3 %pack_round.15 = (f32[12,128,128]{2,1,0:T(8,128)}, f32[12,128,128]{2,1,0:T(8,128)}) custom-call(s32[24]{0:T(128)} %reshape.1693.index_ref, f32[64,128,128]{2,1,0:T(8,128)} %all-to-all-done.1.refs_0_, f32[12,128,128]{2,1,0:T(8,128)S(1)} %collective-permute-done.7.refs_1_, f32[12,128,128]{2,1,0:T(8,128)S(1)} %collective-permute-done.8.refs_2_, ...), custom_call_target="tpu_custom_call" | custom-call | tf_op jit(solution)/shard_map/pack_round/pallas_call | solution.py:159
  181.7 4.4 %collective-permute-done.17.refs_11_.refs_10_.refs_12_ = f32[12,128,128]{2,1,0:T(8,128)} collective-permute-done((f32[12,128,128]{2,1,0:T(8,128)}, f32[12,128,128]{2,1,0:T(8,128)}, u32[]{:S(2)}, u32[]{:S(2)}) %collective-permute-start.17) | collective-permute-done | bytes 786464 | tf_op jit(solution)/shard_map/ppermute | solution.py:563
  186.1 4.3 %pack_round.17 = (f32[12,128,128]{2,1,0:T(8,128)}, f32[12,128,128]{2,1,0:T(8,128)}) custom-call(s32[24]{0:T(128)} %reshape.1695.index_ref, f32[64,128,128]{2,1,0:T(8,128)} %all-to-all-done.1.refs_0_, f32[12,128,128]{2,1,0:T(8,128)S(1)} %collective-permute-done.7.refs_1_, f32[12,128,128]{2,1,0:T(8,128)S(1)} %collective-permute-done.8.refs_2_, ...), custom_call_target="tpu_custom_call" | custom-call | tf_op jit(solution)/shard_map/pack_round/pallas_call | solution.py:159
  190.4 3.5 %collective-permute-start.21 = (f32[12,128,128]{2,1,0:T(8,128)}, f32[12,128,128]{2,1,0:T(8,128)}, u32[]{:S(2)}, u32[]{:S(2)}) collective-permute-start(f32[12,128,128]{2,1,0:T(8,128)} %get-tuple-element.610), channel_id=1, source_target_pairs={{0,8},{8,16},{16,24},{1,9},{9,17},{17,25},{2,10},{10,18},{18,26},{... | collective-permute-start | bytes 2359304 | tf_op jit(solution)/shard_map/ppermute | solution.py:563
  198.5 4.4 %collective-permute-done.18.refs_12_.refs_13_ = f32[12,128,128]{2,1,0:T(8,128)} collective-permute-done((f32[12,128,128]{2,1,0:T(8,128)}, f32[12,128,128]{2,1,0:T(8,128)}, u32[]{:S(2)}, u32[]{:S(2)}) %collective-permute-start.18) | collective-permute-done | bytes 786464 | tf_op jit(solution)/shard_map/ppermute | solution.py:563
  202.9 4.3 %pack_round.16 = (f32[12,128,128]{2,1,0:T(8,128)}, f32[12,128,128]{2,1,0:T(8,128)}) custom-call(s32[24]{0:T(128)} %reshape.1687.index_ref, f32[64,128,128]{2,1,0:T(8,128)} %all-to-all-done.1.refs_0_, f32[12,128,128]{2,1,0:T(8,128)S(1)} %collective-permute-done.7.refs_1_, f32[12,128,128]{2,1,0:T(8,128)S(1)} %collective-permute-done.8.refs_2_, ...), custom_call_target="tpu_custom_call" | custom-call | tf_op jit(solution)/shard_map/pack_round/pallas_call | solution.py:159
  207.3 4.2 %collective-permute-start.19 = (f32[12,128,128]{2,1,0:T(8,128)}, f32[12,128,128]{2,1,0:T(8,128)}, u32[]{:S(2)}, u32[]{:S(2)}) collective-permute-start(f32[12,128,128]{2,1,0:T(8,128)} %get-tuple-element.608), channel_id=1, source_target_pairs={{0,8},{8,16},{16,24},{1,9},{9,17},{17,25},{2,10},{10,18},{18,26},{... | collective-permute-start | bytes 2359304 | tf_op jit(solution)/shard_map/ppermute | solution.py:563
  219.8 23.0 %multiply.7 = f32[96,128,128]{2,1,0:T(8,128)} custom-call(s32[768]{0:T(1024)} %broadcast_add_fusion.8.list_ref, s32[1]{0:T(128)} %bitcast.39.count_ref, f32[264,128,128]{2,1,0:T(8,128)} %all-gather.2.cloned.1.call-done.a_ref, f32[64,128,128]{2,1,0:T(8,128)} %all-to-all-done.1.refs_0_, f32[12,128,128]{2,1,0:T(8,128)S(1)} %collective-permute-done.7.refs_1_, ...), custom_call_target="tpu_custom_call" | custom-call | flops 1887436800 | bytes 67108864 | tf_op jit(solution)/shard_map/multiply/pallas_call | solution.py:338
  242.9 5.3 %conditional.1 = (f32[16,6,128,128]{3,2,1,0:T(8,128)S(1)}) conditional(s32[]{:T(128)} %clamp.3, (s32[768]{0:T(1024)S(1)}, s32[1]{0:T(128)}, f32[264,128,128]{2,1,0:T(8,128)}, f32[12,128,128]{2,1,0:T(8,128)}, f32[12,128,128]{2,1,0:T(8,128)}, /*index=5*/f32[96,128,128]{2,1,0:T(8,128)}) %tuple.60, (s32[2,120]{1,0:T(2,128)S(1)}, ...), branch_computations={%region_28.32_spmd, %region_29.33_spmd, %region_30.55_spmd} | conditional | flops 1895540480 | bytes 102514648 | solution.py:624
  242.9 5.0 %multiply.4 = f32[96,128,128]{2,1,0:T(8,128)S(1)} custom-call(s32[768]{0:T(1024)S(1)} %get-tuple-element.486.list_ref, s32[1]{0:T(128)} %get-tuple-element.487.count_ref, f32[264,128,128]{2,1,0:T(8,128)} %get-tuple-element.488.a_ref, f32[12,128,128]{2,1,0:T(8,128)} %get-tuple-element.489.refs_0_.refs_1_, f32[12,128,128]{2,1,0:T(8,128)} %get-tuple-element.489.refs_0_.refs_1_, ...), custom_call_target="tpu_custom_call" | custom-call | flops 1887436800 | bytes 67108864 | tf_op jit(solution)/shard_map/cond/branch_0_fun/multiply/pallas_call | solution.py:338
  (225 shorter events, 66.2 us)
Async XLA Ops:
  10.1 14.3 %all-to-all-start = ((s32[32,1,192]{2,1,0:T(1,128)}), s32[32,1,192]{2,1,0:T(1,128)S(1)}, u32[]{:S(2)}, u32[]{:S(2)}) async-start(s32[32,1,192]{2,1,0:T(1,128)} %broadcast_in_dim.719), calls=%async_computation | async-start | bytes 65536 | tf_op jit(solution)/shard_map/all_to_all | solution.py:37
  24.4 12.7 %copy-start.20 = (f32[8,128,128]{2,1,0:T(8,128)S(1)}, f32[8,128,128]{2,1,0:T(8,128)}, u32[]{:S(2)}) copy-start(f32[8,128,128]{2,1,0:T(8,128)} %get-tuple-element.587) | copy-start | bytes 1572868
  24.4 14.0 %copy-start.6 = (s32[2,256]{1,0:T(2,128)S(1)}, s32[2,256]{1,0:T(2,128)}, u32[]{:S(2)}) copy-start(s32[2,256]{1,0:T(2,128)} %constant.933.clone..sunk.3) | copy-start | bytes 6148
  24.4 14.0 %copy-start.8 = (s32[2,256]{1,0:T(2,128)S(1)}, s32[2,256]{1,0:T(2,128)}, u32[]{:S(2)}) copy-start(s32[2,256]{1,0:T(2,128)} %constant.1381) | copy-start | bytes 6148
  24.4 14.0 %copy-start.9 = (pred[2,1,256]{2,1,0:T(4,128)(4,1)S(1)}, pred[2,1,256]{2,1,0:T(4,128)(4,1)}, u32[]{:S(2)}) copy-start(pred[2,1,256]{2,1,0:T(4,128)(4,1)} %constant.1380) | copy-start | bytes 1540
  24.4 14.0 %copy-start.10 = (pred[2,1,256]{2,1,0:T(4,128)(4,1)S(1)}, pred[2,1,256]{2,1,0:T(4,128)(4,1)}, u32[]{:S(2)}) copy-start(pred[2,1,256]{2,1,0:T(4,128)(4,1)} %constant.1379) | copy-start | bytes 1540
  24.4 14.0 %copy-start.12 = (s32[256]{0:T(256)S(1)}, s32[256]{0:T(256)}, u32[]{:S(2)}) copy-start(s32[256]{0:T(256)} %constant.932.clone..sunk.3) | copy-start | bytes 3076
  24.5 14.0 %copy-start.13 = (s32[1,256]{1,0:T(1,128)S(1)}, s32[1,256]{1,0:T(1,128)}, u32[]{:S(2)}) copy-start(s32[1,256]{1,0:T(1,128)} %constant.1382) | copy-start | bytes 3076
  24.5 52.5 %all-to-all-start.1 = ((f32[64,128,128]{2,1,0:T(8,128)}), f32[64,128,128]{2,1,0:T(8,128)}, u32[]{:S(2)}, u32[]{:S(2)}) async-start(f32[64,128,128]{2,1,0:T(8,128)} %get-tuple-element.580), calls=%async_computation.1 | async-start | bytes 8388608 | tf_op jit(solution)/shard_map/all_to_all | solution.py:416
  29.3 185.9 %all-gather.2.cloned.1.call-start = ((), (), s32[]{:S(2)}) async-start(), calls=%async_computation.2 | async-start | bytes 19464192 | tf_op jit(solution)/shard_map/all_gather | solution.py:554
  32.8 24.9 %collective-permute-start.4 = (f32[8,128,128]{2,1,0:T(8,128)}, f32[8,128,128]{2,1,0:T(8,128)S(1)}, u32[]{:S(2)}, u32[]{:S(2)}) collective-permute-start(f32[8,128,128]{2,1,0:T(8,128)} %get-tuple-element.585), channel_id=1, source_target_pairs={{0,8},{8,0},{16,24},{24,16},{1,9},{9,1},{17,25},{25,17},{2,10},{10... | collective-permute-start | bytes 1572872 | tf_op jit(solution)/shard_map/ppermute | solution.py:31
  34.7 38.4 %collective-permute-start.5 = (f32[8,128,128]{2,1,0:T(8,128)}, f32[8,128,128]{2,1,0:T(8,128)S(1)}, u32[]{:S(2)}, u32[]{:S(2)}) collective-permute-start(f32[8,128,128]{2,1,0:T(8,128)} %get-tuple-element.586), channel_id=1, source_target_pairs={{0,16},{8,24},{16,0},{24,8},{1,17},{9,25},{17,1},{25,9},{2,18},{10... | collective-permute-start | bytes 1572872 | tf_op jit(solution)/shard_map/ppermute | solution.py:31
  37.1 36.0 %collective-permute-start.6 = (f32[8,128,128]{2,1,0:T(8,128)S(1)}, f32[8,128,128]{2,1,0:T(8,128)S(1)}, u32[]{:S(2)}, u32[]{:S(2)}) collective-permute-start(f32[8,128,128]{2,1,0:T(8,128)S(1)} %copy-done.20), channel_id=1, source_target_pairs={{0,24},{8,16},{16,8},{24,0},{1,25},{9,17},{17,9},{25,1},{2,26},{10... | collective-permute-start | bytes 1572872 | tf_op jit(solution)/shard_map/ppermute | solution.py:31
  57.7 19.9 %copy-start.3 = (f32[8,128,128]{2,1,0:T(8,128)}, f32[8,128,128]{2,1,0:T(8,128)S(1)}, u32[]{:S(2)}) copy-start(f32[8,128,128]{2,1,0:T(8,128)S(1)} %collective-permute-done.4.refs_1_) | copy-start | bytes 1572868
  73.1 4.6 %copy-start.4 = (f32[8,128,128]{2,1,0:T(8,128)}, f32[8,128,128]{2,1,0:T(8,128)S(1)}, u32[]{:S(2)}) copy-start(f32[8,128,128]{2,1,0:T(8,128)S(1)} %collective-permute-done.5.refs_2_) | copy-start | bytes 1572868
  87.7 19.3 %copy-start.18 = (s32[256]{0:T(256)S(1)}, s32[256]{0:T(256)}, u32[]{:S(2)}) copy-start(s32[256]{0:T(256)} %get-tuple-element.593) | copy-start | bytes 3076
  87.7 26.5 %collective-permute-start.7 = (f32[12,128,128]{2,1,0:T(8,128)}, f32[12,128,128]{2,1,0:T(8,128)S(1)}, u32[]{:S(2)}, u32[]{:S(2)}) collective-permute-start(f32[12,128,128]{2,1,0:T(8,128)} %get-tuple-element.596), channel_id=1, source_target_pairs={{0,8},{8,16},{16,24},{1,9},{9,17},{17,25},{2,10},{10,18},{18,26},{... | collective-permute-start | bytes 2359304 | tf_op jit(solution)/shard_map/ppermute | solution.py:563
  96.0 22.6 %collective-permute-start.9 = (f32[12,128,128]{2,1,0:T(8,128)}, f32[12,128,128]{2,1,0:T(8,128)S(1)}, u32[]{:S(2)}, u32[]{:S(2)}) collective-permute-start(f32[12,128,128]{2,1,0:T(8,128)} %get-tuple-element.598), channel_id=1, source_target_pairs={{8,0},{16,8},{24,16},{9,1},{17,9},{25,17},{10,2},{18,10},{26,18},{... | collective-permute-start | bytes 2359304 | tf_op jit(solution)/shard_map/ppermute | solution.py:563
  101.7 29.4 %collective-permute-start.8 = (f32[12,128,128]{2,1,0:T(8,128)}, f32[12,128,128]{2,1,0:T(8,128)S(1)}, u32[]{:S(2)}, u32[]{:S(2)}) collective-permute-start(f32[12,128,128]{2,1,0:T(8,128)} %get-tuple-element.597), channel_id=1, source_target_pairs={{0,8},{8,16},{16,24},{1,9},{9,17},{17,25},{2,10},{10,18},{18,26},{... | collective-permute-start | bytes 2359304 | tf_op jit(solution)/shard_map/ppermute | solution.py:563
  105.7 29.7 %collective-permute-start.11 = (f32[12,128,128]{2,1,0:T(8,128)}, f32[12,128,128]{2,1,0:T(8,128)S(1)}, u32[]{:S(2)}, u32[]{:S(2)}) collective-permute-start(f32[12,128,128]{2,1,0:T(8,128)} %get-tuple-element.600), channel_id=1, source_target_pairs={{8,0},{16,8},{24,16},{9,1},{17,9},{25,17},{10,2},{18,10},{26,18},{... | collective-permute-start | bytes 2359304 | tf_op jit(solution)/shard_map/ppermute | solution.py:563
  122.3 25.6 %collective-permute-start.10 = (f32[12,128,128]{2,1,0:T(8,128)}, f32[12,128,128]{2,1,0:T(8,128)}, u32[]{:S(2)}, u32[]{:S(2)}) collective-permute-start(f32[12,128,128]{2,1,0:T(8,128)} %get-tuple-element.599), channel_id=1, source_target_pairs={{0,8},{8,16},{16,24},{1,9},{9,17},{17,25},{2,10},{10,18},{18,26},{... | collective-permute-start | bytes 2359304 | tf_op jit(solution)/shard_map/ppermute | solution.py:563
  127.3 25.1 %collective-permute-start.13 = (f32[12,128,128]{2,1,0:T(8,128)}, f32[12,128,128]{2,1,0:T(8,128)}, u32[]{:S(2)}, u32[]{:S(2)}) collective-permute-start(f32[12,128,128]{2,1,0:T(8,128)} %get-tuple-element.602), channel_id=1, source_target_pairs={{8,0},{16,8},{24,16},{9,1},{17,9},{25,17},{10,2},{18,10},{26,18},{... | collective-permute-start | bytes 2359304 | tf_op jit(solution)/shard_map/ppermute | solution.py:563
  139.2 25.6 %collective-permute-start.12 = (f32[12,128,128]{2,1,0:T(8,128)}, f32[12,128,128]{2,1,0:T(8,128)}, u32[]{:S(2)}, u32[]{:S(2)}) collective-permute-start(f32[12,128,128]{2,1,0:T(8,128)} %get-tuple-element.601), channel_id=1, source_target_pairs={{0,8},{8,16},{16,24},{1,9},{9,17},{17,25},{2,10},{10,18},{18,26},{... | collective-permute-start | bytes 2359304 | tf_op jit(solution)/shard_map/ppermute | solution.py:563
  144.3 24.9 %collective-permute-start.15 = (f32[12,128,128]{2,1,0:T(8,128)}, f32[12,128,128]{2,1,0:T(8,128)}, u32[]{:S(2)}, u32[]{:S(2)}) collective-permute-start(f32[12,128,128]{2,1,0:T(8,128)} %get-tuple-element.604), channel_id=1, source_target_pairs={{8,0},{16,8},{24,16},{9,1},{17,9},{25,17},{10,2},{18,10},{26,18},{... | collective-permute-start | bytes 2359304 | tf_op jit(solution)/shard_map/ppermute | solution.py:563
  156.6 25.0 %collective-permute-start.14 = (f32[12,128,128]{2,1,0:T(8,128)}, f32[12,128,128]{2,1,0:T(8,128)}, u32[]{:S(2)}, u32[]{:S(2)}) collective-permute-start(f32[12,128,128]{2,1,0:T(8,128)} %get-tuple-element.603), channel_id=1, source_target_pairs={{0,8},{8,16},{16,24},{1,9},{9,17},{17,25},{2,10},{10,18},{18,26},{... | collective-permute-start | bytes 2359304 | tf_op jit(solution)/shard_map/ppermute | solution.py:563
  159.8 26.3 %collective-permute-start.17 = (f32[12,128,128]{2,1,0:T(8,128)}, f32[12,128,128]{2,1,0:T(8,128)}, u32[]{:S(2)}, u32[]{:S(2)}) collective-permute-start(f32[12,128,128]{2,1,0:T(8,128)} %get-tuple-element.606), channel_id=1, source_target_pairs={{8,0},{16,8},{24,16},{9,1},{17,9},{25,17},{10,2},{18,10},{26,18},{... | collective-permute-start | bytes 2359304 | tf_op jit(solution)/shard_map/ppermute | solution.py:563
  173.6 25.0 %collective-permute-start.16 = (f32[12,128,128]{2,1,0:T(8,128)}, f32[12,128,128]{2,1,0:T(8,128)}, u32[]{:S(2)}, u32[]{:S(2)}) collective-permute-start(f32[12,128,128]{2,1,0:T(8,128)} %get-tuple-element.605), channel_id=1, source_target_pairs={{0,8},{8,16},{16,24},{1,9},{9,17},{17,25},{2,10},{10,18},{18,26},{... | collective-permute-start | bytes 2359304 | tf_op jit(solution)/shard_map/ppermute | solution.py:563
  176.6 26.3 %collective-permute-start.18 = (f32[12,128,128]{2,1,0:T(8,128)}, f32[12,128,128]{2,1,0:T(8,128)}, u32[]{:S(2)}, u32[]{:S(2)}) collective-permute-start(f32[12,128,128]{2,1,0:T(8,128)} %get-tuple-element.607), channel_id=1, source_target_pairs={{8,0},{16,8},{24,16},{9,1},{17,9},{25,17},{10,2},{18,10},{26,18},{... | collective-permute-start | bytes 2359304 | tf_op jit(solution)/shard_map/ppermute | solution.py:563
  190.4 26.8 %collective-permute-start.21 = (f32[12,128,128]{2,1,0:T(8,128)}, f32[12,128,128]{2,1,0:T(8,128)}, u32[]{:S(2)}, u32[]{:S(2)}) collective-permute-start(f32[12,128,128]{2,1,0:T(8,128)} %get-tuple-element.610), channel_id=1, source_target_pairs={{0,8},{8,16},{16,24},{1,9},{9,17},{17,25},{2,10},{10,18},{18,26},{... | collective-permute-start | bytes 2359304 | tf_op jit(solution)/shard_map/ppermute | solution.py:563
  193.9 25.9 %collective-permute-start.22 = (f32[12,128,128]{2,1,0:T(8,128)}, f32[12,128,128]{2,1,0:T(8,128)}, u32[]{:S(2)}, u32[]{:S(2)}) collective-permute-start(f32[12,128,128]{2,1,0:T(8,128)} %get-tuple-element.611), channel_id=1, source_target_pairs={{8,0},{16,8},{24,16},{9,1},{17,9},{25,17},{10,2},{18,10},{26,18},{... | collective-permute-start | bytes 2359304 | tf_op jit(solution)/shard_map/ppermute | solution.py:563
  207.3 35.6 %collective-permute-start.19 = (f32[12,128,128]{2,1,0:T(8,128)}, f32[12,128,128]{2,1,0:T(8,128)}, u32[]{:S(2)}, u32[]{:S(2)}) collective-permute-start(f32[12,128,128]{2,1,0:T(8,128)} %get-tuple-element.608), channel_id=1, source_target_pairs={{0,8},{8,16},{16,24},{1,9},{9,17},{17,25},{2,10},{10,18},{18,26},{... | collective-permute-start | bytes 2359304 | tf_op jit(solution)/shard_map/ppermute | solution.py:563
  211.5 31.4 %collective-permute-start.20 = (f32[12,128,128]{2,1,0:T(8,128)}, f32[12,128,128]{2,1,0:T(8,128)}, u32[]{:S(2)}, u32[]{:S(2)}) collective-permute-start(f32[12,128,128]{2,1,0:T(8,128)} %get-tuple-element.609), channel_id=1, source_target_pairs={{8,0},{16,8},{24,16},{9,1},{17,9},{25,17},{10,2},{18,10},{26,18},{... | collective-permute-start | bytes 2359304 | tf_op jit(solution)/shard_map/ppermute | solution.py:563
  (4 other events, 13.6 us)
Sparse Core Ops, SparseCore 0:
  80.2 97.5 all-gather.1
